TPU v7x, 256 devices: a whole 4x4x8 slice. The times are simulated.
256 devices in a mesh: dp: 8 (over z), tensor: 16 (over y, x), group: 2 (over core).
Axes of the slice: x: 4, y: 4, z: 8, core: 2. Of those that a mesh axis runs over, the one named last changes fastest.
Arguments:
- resid: bfloat16 [1024, 4096], P('dp'), may hold values from -6 to 6
- mixer_out: bfloat16 [1024, 8192], P('dp', ('tensor', 'group')), may hold values from -6 to 6
- out_proj: bfloat16 [8192, 4096], P(('tensor', 'group')), may hold values from -0.0625 to 0.0625
- norm_gain: float32 [4096], replicated, may hold values from 0.1 to 1.9
- router: float32 [4096, 8], replicated, may hold values from -0.09375 to 0.09375
- routes: int32 [1024, 2], P('dp'), may hold values from 0 to 7, all different within a row; in each aligned block of 128 rows (0 to 127, 128 to 255, ...) at most 48 rows name the same one
- w_gate: bfloat16 [16, 4096, 3584], P('tensor', None, ('dp', 'group')), may hold values from -0.09375 to 0.09375
- w_up: bfloat16 [16, 4096, 3584], P('tensor', None, ('dp', 'group')), may hold values from -0.09375 to 0.09375
- w_down: bfloat16 [16, 3584, 4096], P('tensor', ('dp', 'group')), may hold values from -0.0625 to 0.0625
- cotangent: bfloat16 [1024, 4096], P('dp'), may hold values from -6 to 6
Outputs:
- layer_out: bfloat16 [1024, 4096], P('dp')
- grad_mixer: bfloat16 [1024, 8192], P('dp', ('tensor', 'group'))
- grad_down: bfloat16 [16, 3584, 4096], P('tensor', ('dp', 'group'))
Inputs may be any that keep to these rules, and one draw needn't show every extreme that they name: `routes`: in each aligned block of 128 rows (the tokens of one replica) no expert is named by more than 48 rows, and some expert reaches 48 in some block; the two experts of a row differ.
All inputs are finite; a program needn't handle non-finite values.
Results may differ from a plain program's by a relative error of at most 0.03.
Values may be sent and summed in bfloat16 or wider, within the bound.
No kernel may reach another device: no remote copies, remote signals or barrier semaphores. Data moves between devices by JAX's collectives and lax.ppermute only.
A program may use at most 128 MiB of HBM per device.

v0:
```python
import jax
import jax.numpy as jnp
from jax import lax
from jax.sharding import Mesh, PartitionSpec as P

BF = jnp.bfloat16
F32 = jnp.float32
CHIPS = ("y", "xh", "half")


def contract_rows(left, right):
    return lax.dot_general(left, right, (((0,), (0,)), ((), ())), preferred_element_type=F32)


def contract_cols(left, right):
    return lax.dot_general(left, right, (((1,), (1,)), ((), ())), preferred_element_type=F32)


def split_three(values):
    high = lax.reduce_precision(values, 8, 7)
    rest = values - high
    mid = lax.reduce_precision(rest, 8, 7)
    low = rest - mid
    return high.astype(BF), mid.astype(BF), low.astype(BF)


def swap_core(value):
    return lax.ppermute(value, "group", [(0, 1), (1, 0)])


def hop(value, size, back):
    pairs = []
    for z in range(size):
        up, down = (z + 1) % size, (z - 1) % size
        if back:
            up, down = down, up
        pairs += [(2 * z, 2 * up), (2 * z + 1, 2 * down + 1)]
    return lax.ppermute(value, ("dp", "group"), pairs)


def exchange(blocks):
    return lax.all_to_all(blocks, CHIPS, 0, 0)


def join_halves(core, mine, other):
    return jnp.where(
        core == 0, jnp.concatenate((mine, other), 1), jnp.concatenate((other, mine), 1)
    )


def gather_features(core, block):
    rows, width = block.shape
    got = exchange(jnp.broadcast_to(block[None], (16, rows, width)))
    other = swap_core(got)
    mine = jnp.transpose(got, (1, 0, 2)).reshape(rows, 16 * width)
    other = jnp.transpose(other, (1, 0, 2)).reshape(rows, 16 * width)
    return join_halves(core, mine, other)


def on_device(
    resid, mixer_out, out_proj, norm_gain, router, routes, w_gate, w_up, w_down, cotangent
):
    rows, width = resid.shape
    experts = router.shape[1]
    units = w_gate.shape[2]
    cap = min(rows, 3 * rows // experts)
    half_width = width // 2
    block = half_width // 16
    z = lax.axis_index("dp")
    core = lax.axis_index("group")
    chip = (lax.axis_index("y") * 2 + lax.axis_index("xh")) * 2 + lax.axis_index("half")
    expert = lax.axis_index("y") * 2 + lax.axis_index("xh")
    first = core * half_width + chip * block

    pair_expert = routes.reshape(-1)
    onehot = (pair_expert[:, None] == jnp.arange(experts, dtype=jnp.int32)[None, :])
    before = jnp.dot(
        (jnp.arange(2 * rows)[:, None] > jnp.arange(2 * rows)[None, :]).astype(BF),
        onehot.astype(BF),
        preferred_element_type=F32,
    )
    slot = jnp.sum(before * onehot.astype(F32), axis=1).astype(jnp.int32)
    target = (pair_expert * cap + slot).reshape(rows, 2)
    own_slots = expert * cap + jnp.arange(cap, dtype=jnp.int32)
    select = (
        (target[None, :, 0] == own_slots[:, None]) | (target[None, :, 1] == own_slots[:, None])
    ).astype(BF)

    own_cots = jnp.dot(select, cotangent, preferred_element_type=F32).astype(BF)
    mixer_out, own_cots = lax.optimization_barrier((mixer_out, own_cots))
    all_cots = lax.all_gather(own_cots, "dp", axis=0)
    term = jnp.dot(mixer_out, out_proj, preferred_element_type=F32).astype(BF)
    sent = lax.dynamic_slice_in_dim(term, (1 - core) * half_width, half_width, 1)
    kept = lax.dynamic_slice_in_dim(term, core * half_width, half_width, 1)
    chip_term = (kept.astype(F32) + swap_core(sent).astype(F32)).astype(BF)
    blocks = exchange(jnp.transpose(chip_term.reshape(rows, 16, block), (1, 0, 2)))
    hidden = lax.dynamic_slice_in_dim(resid, first, block, 1).astype(F32) + jnp.sum(
        blocks.astype(F32), axis=0
    )
    whole = gather_features(core, hidden.astype(BF)).astype(F32)
    inv_rms = lax.rsqrt(jnp.mean(whole * whole, axis=1, keepdims=True) + 1e-05)
    normed = (whole * inv_rms * norm_gain).astype(BF)
    own_rows = jnp.dot(select, normed, preferred_element_type=F32).astype(BF)

    own_rows, all_cots = lax.optimization_barrier((own_rows, all_cots))
    near = [own_rows]
    for _ in range(3):
        near.append(hop(near[-1], 8, False))
    far = hop(
        lax.dynamic_slice_in_dim(near[3], core * half_width, half_width, 1), 8, False
    )
    others = [swap_core(value) for value in near[1:]]
    far = join_halves(core, far, swap_core(far))
    inputs = jnp.concatenate(near + others + [far], axis=0)
    sign = 1 - 2 * core
    order = [z, z - sign, z - 2 * sign, z - 3 * sign, z + sign, z + 2 * sign, z + 3 * sign, z + 4]
    cots = jnp.concatenate(
        [lax.dynamic_index_in_dim(all_cots, (place + 8) % 8, 0, False) for place in order], axis=0
    )

    own_router = lax.dynamic_index_in_dim(router.T, expert, 0, True)
    r_high, r_mid, r_low = split_three(own_router)
    logit = jnp.sum(
        contract_cols(inputs, jnp.concatenate((r_high, r_mid, r_low), 0)), axis=1, keepdims=True
    )
    gate = jax.nn.sigmoid(logit)
    pre_gate = jnp.dot(inputs, w_gate[0], preferred_element_type=F32)
    pre_up = jnp.dot(inputs, w_up[0], preferred_element_type=F32)
    sig = jax.nn.sigmoid(pre_gate)
    activated = (pre_gate * sig * pre_up).astype(BF)
    out_part = jnp.dot(activated, w_down[0], preferred_element_type=F32).astype(BF)
    out_cot = (gate * cots.astype(F32)).astype(BF)
    act_cot = contract_cols(out_cot, w_down[0])
    d_gate = (act_cot * pre_up * sig * (1.0 + pre_gate * (1.0 - sig))).astype(BF)
    d_up = (act_cot * pre_gate * sig).astype(BF)
    gate_term = (1.0 - gate) * jnp.sum(activated.astype(F32) * act_cot, axis=1, keepdims=True)
    in_part = (
        contract_cols(d_gate, w_gate[0]) + contract_cols(d_up, w_up[0]) + gate_term * own_router
    ).astype(BF)
    grad_down = contract_rows(activated, out_cot).astype(BF)[None]

    def collect(part):
        parts = part.reshape(8, cap, width)
        far_sent = lax.dynamic_slice_in_dim(parts[7], (1 - core) * half_width, half_width, 1)
        far_kept = lax.dynamic_slice_in_dim(parts[7], core * half_width, half_width, 1)
        total = (far_kept.astype(F32) + swap_core(far_sent).astype(F32)).astype(BF)
        total = hop(total, 8, True).astype(F32)
        nothing = jnp.zeros_like(total)
        total = join_halves(core, total, nothing)
        for place in (3, 2, 1):
            total = total + parts[place].astype(F32) + swap_core(parts[place + 3]).astype(F32)
            total = hop(total.astype(BF), 8, True).astype(F32)
        total = (total + parts[0].astype(F32)).astype(BF)
        return total.astype(F32) + swap_core(total).astype(F32)

    half_out = collect(out_part)
    half_in = collect(in_part)

    own_gate = gate[:cap]
    mean_part = jnp.sum(half_in * own_rows.astype(F32), axis=1)
    mean_high = lax.reduce_precision(mean_part, 8, 7)
    mean_low = mean_part - mean_high
    scaled = (own_gate * half_out).astype(BF)
    both = jnp.concatenate((scaled, half_in.astype(BF)), axis=0)
    both = lax.dynamic_slice_in_dim(both, core * half_width, half_width, 1)
    both = jnp.transpose(both.reshape(2 * cap, 16, block), (1, 0, 2))
    means = jnp.concatenate((mean_high, mean_low, jnp.zeros((block - 2 * cap,), F32))).astype(BF)
    message = jnp.concatenate(
        (both, jnp.broadcast_to(means[None, None], (16, 16, block))), axis=1
    )
    got = exchange(message)
    places = jnp.arange(experts * cap, dtype=jnp.int32)
    spread = (
        (target[:, :1] == places[None, :]) | (target[:, 1:] == places[None, :])
    ).reshape(rows, experts, 1, cap)
    spread = jnp.broadcast_to(spread, (rows, experts, 2, cap)).reshape(rows, 16 * cap)
    mixture = jnp.dot(
        spread.astype(BF), got[:, :cap].reshape(16 * cap, block), preferred_element_type=F32
    )
    normed_cot = jnp.dot(
        spread.astype(BF),
        got[:, cap : 2 * cap].reshape(16 * cap, block),
        preferred_element_type=F32,
    )
    means = got[:, 2 * cap, :cap].astype(F32) + got[:, 2 * cap, cap : 2 * cap].astype(F32)
    inner = jnp.sum(spread.astype(F32) * means.reshape(1, 16 * cap), axis=1, keepdims=True)
    gain_here = lax.dynamic_slice_in_dim(norm_gain, first, block, 0)
    cot_here = lax.dynamic_slice_in_dim(cotangent, first, block, 1).astype(F32)
    layer_here = (hidden + mixture).astype(BF)
    cot_out = (
        cot_here
        + inv_rms * (normed_cot * gain_here)
        - inv_rms * inv_rms * hidden * (inner / width)
    ).astype(BF)
    final = gather_features(core, jnp.concatenate((layer_here, cot_out), axis=0))
    layer_out = final[:rows]
    grad_mixer = contract_cols(final[rows:], out_proj).astype(BF)
    return (layer_out, grad_mixer, grad_down)


def solution(mesh):
    fine = Mesh(mesh.devices.reshape(8, 4, 2, 2, 2), ("dp", "y", "xh", "half", "group"))
    tensor = ("y", "xh", "half")
    plane = tensor + ("group",)
    slices = ("dp", "group")
    placed = (
        P("dp", None),
        P("dp", plane),
        P(plane, None),
        P(),
        P(),
        P("dp", None),
        P(tensor, None, slices),
        P(tensor, None, slices),
        P(tensor, slices, None),
        P("dp", None),
    )
    return jax.shard_map(
        on_device,
        mesh=fine,
        in_specs=placed,
        out_specs=(P("dp", None), P("dp", plane), P(tensor, slices, None)),
        check_vma=False,
    )
```

profile of v0, /device:TPU:1, one launch (start us, length us, event | category | flops | bytes accessed | tf_op | source)
XLA Modules:
  0.0 209.9 jit_solution(16096691444682781401)
XLA Ops:
  7.2 0.9 copy.36
  8.7 0.7 multiply_add_fusion.1
  9.4 2.3 %convolution_convert_fusion.4 = bf16[48,4096]{1,0:T(8,128)(2,1)} fusion(bf16[128,4096]{1,0:T(8,128)(2,1)} %param.19, s32[128]{0:T(128)S(1)} %get-tuple-element.36, s32[128]{0:T(128)S(1)} %get-tuple-element.35, s32[48]{0:T(128)S(1)} %iota_add_fusion), kind=kOutput, calls=%fused_computation.7 | convolution fusion | flops 50546688 | bytes 1443008 | tf_op jit(solution)/shard_map/dot_general | solution.py:89
  11.8 1.3 convolution_convert_fusion.2
  13.1 0.8 constant_dynamic-slice_fusion.4
  13.9 3.2 %collective-permute-start = (bf16[128,2048]{1,0:T(8,128)(2,1)}, bf16[128,2048]{1,0:T(8,128)(2,1)}, u32[]{:S(2)}, u32[]{:S(2)}) collective-permute-start(bf16[128,2048]{1,0:T(8,128)(2,1)} %constant_dynamic-slice_fusion.4), channel_id=1, source_target_pairs={{0,1},{1,0},{2,3},{3,2},{4,5},{5,4},{6,7},{7,6},{8,9},{9,8},{10,11... | collective-permute-start | bytes 1572872 | tf_op jit(solution)/shard_map/ppermute | solution.py:28
  17.2 1.9 collective-permute-done
  19.0 2.0 bitcast_bitcast_fusion
  21.0 5.1 %all-to-all-start = ((bf16[16,128,128]{2,1,0:T(8,128)(2,1)}), bf16[16,128,128]{2,1,0:T(8,128)(2,1)S(1)}, u32[]{:S(2)}, u32[]{:S(2)}) async-start(bf16[16,128,128]{2,1,0:T(8,128)(2,1)} %bitcast_bitcast_fusion), calls=%async_computation | async-start | bytes 1048576 | tf_op jit(solution)/shard_map/all_to_all | solution.py:42
  26.2 10.7 %all-to-all-done = bf16[16,128,128]{2,1,0:T(8,128)(2,1)S(1)} async-done(((bf16[16,128,128]{2,1,0:T(8,128)(2,1)}), bf16[16,128,128]{2,1,0:T(8,128)(2,1)S(1)}, u32[]{:S(2)}, u32[]{:S(2)}) %all-to-all-start) | async-done | bytes 524320 | tf_op jit(solution)/shard_map/all_to_all | solution.py:42
  37.0 0.8 fusion.36
  37.7 0.9 broadcast_in_dim.13
  38.6 3.6 %all-to-all-start.1 = ((bf16[16,128,128]{2,1,0:T(8,128)(2,1)}), bf16[16,128,128]{2,1,0:T(8,128)(2,1)S(1)}, u32[]{:S(2)}, u32[]{:S(2)}) async-start(bf16[16,128,128]{2,1,0:T(8,128)(2,1)} %broadcast_in_dim.13), calls=%async_computation.1 | async-start | bytes 1048576 | tf_op jit(solution)/shard_map/all_to_all | solution.py:42
  42.3 0.9 reduce-precision_convert_fusion.1
  43.3 9.0 %all-to-all-done.1 = bf16[16,128,128]{2,1,0:T(8,128)(2,1)S(1)} async-done(((bf16[16,128,128]{2,1,0:T(8,128)(2,1)}), bf16[16,128,128]{2,1,0:T(8,128)(2,1)S(1)}, u32[]{:S(2)}, u32[]{:S(2)}) %all-to-all-start.1) | async-done | bytes 524320 | tf_op jit(solution)/shard_map/all_to_all | solution.py:42
  52.5 2.6 %collective-permute-start.1 = (bf16[16,128,128]{1,2,0:T(8,128)(2,1)S(1)}, bf16[16,128,128]{1,2,0:T(8,128)(2,1)S(1)}, u32[]{:S(2)}, u32[]{:S(2)}) collective-permute-start(bf16[16,128,128]{1,2,0:T(8,128)(2,1)S(1)} %copy.39), channel_id=1, source_target_pairs={{0,1},{1,0},{2,3},{3,2},{4,5},{5,4},{6,7},{7,6},{8,9},{9,8},{10,11... | collective-permute-start | bytes 1572872 | tf_op jit(solution)/shard_map/ppermute | solution.py:28
  55.1 1.5 collective-permute-done.1
  56.6 0.6 fusion.1
  57.2 0.8 convolution_convert_fusion.3
  58.0 2.5 %all-gather.3.cloned.1.call-done = bf16[384,4096]{1,0:T(8,128)(2,1)} async-done(((bf16[48,4096]{1,0:T(8,128)(2,1)}), bf16[384,4096]{1,0:T(8,128)(2,1)}) %all-gather.3.cloned.1.call-update) | async-done | bytes 3145744 | tf_op jit(solution)/shard_map/all_gather | solution.py:91
  60.5 3.2 %collective-permute-start.2 = (bf16[48,4096]{1,0:T(8,128)(2,1)S(1)}, bf16[48,4096]{1,0:T(8,128)(2,1)S(1)}, u32[]{:S(2)}, u32[]{:S(2)}) collective-permute-start(bf16[48,4096]{1,0:T(8,128)(2,1)S(1)} %convolution_convert_fusion.3), channel_id=1, source_target_pairs={{0,32},{1,225},{32,64},{33,1},{64,96},{65,33},{96,128},{97,65},{12... | collective-permute-start | bytes 1179656 | tf_op jit(solution)/shard_map/ppermute | solution.py:38
  63.7 1.0 bitcast_dynamic-update-slice_fusion.7
  64.7 1.0 bitcast_dynamic-update-slice_fusion.6
  65.8 1.0 bitcast_dynamic-update-slice_fusion.5
  66.8 1.0 bitcast_dynamic-update-slice_fusion.4
  68.4 3.1 %collective-permute-start.3 = (bf16[48,4096]{1,0:T(8,128)(2,1)S(1)}, bf16[48,4096]{1,0:T(8,128)(2,1)S(1)}, u32[]{:S(2)}, u32[]{:S(2)}) collective-permute-start(bf16[48,4096]{1,0:T(8,128)(2,1)S(1)} %collective-permute-done.2), channel_id=1, source_target_pairs={{0,32},{1,225},{32,64},{33,1},{64,96},{65,33},{96,128},{97,65},{12... | collective-permute-start | bytes 1179656 | tf_op jit(solution)/shard_map/ppermute | solution.py:38
  71.6 4.7 %collective-permute-done.3 = bf16[48,4096]{1,0:T(8,128)(2,1)S(1)} collective-permute-done((bf16[48,4096]{1,0:T(8,128)(2,1)S(1)}, bf16[48,4096]{1,0:T(8,128)(2,1)S(1)}, u32[]{:S(2)}, u32[]{:S(2)}) %collective-permute-start.3) | collective-permute-done | bytes 393248 | tf_op jit(solution)/shard_map/ppermute | solution.py:38
  76.3 3.1 %collective-permute-start.4 = (bf16[48,4096]{1,0:T(8,128)(2,1)S(1)}, bf16[48,4096]{1,0:T(8,128)(2,1)S(1)}, u32[]{:S(2)}, u32[]{:S(2)}) collective-permute-start(bf16[48,4096]{1,0:T(8,128)(2,1)S(1)} %collective-permute-done.3), channel_id=1, source_target_pairs={{0,32},{1,225},{32,64},{33,1},{64,96},{65,33},{96,128},{97,65},{12... | collective-permute-start | bytes 1179656 | tf_op jit(solution)/shard_map/ppermute | solution.py:38
  79.4 4.7 %collective-permute-done.4 = bf16[48,4096]{1,0:T(8,128)(2,1)S(1)} collective-permute-done((bf16[48,4096]{1,0:T(8,128)(2,1)S(1)}, bf16[48,4096]{1,0:T(8,128)(2,1)S(1)}, u32[]{:S(2)}, u32[]{:S(2)}) %collective-permute-start.4) | collective-permute-done | bytes 393248 | tf_op jit(solution)/shard_map/ppermute | solution.py:38
  84.1 3.2 %collective-permute-start.8 = (bf16[48,2048]{1,0:T(8,128)(2,1)S(1)}, bf16[48,2048]{1,0:T(8,128)(2,1)S(1)}, u32[]{:S(2)}, u32[]{:S(2)}) collective-permute-start(bf16[48,2048]{1,0:T(8,128)(2,1)S(1)} %constant_dynamic-slice_fusion.3), channel_id=1, source_target_pairs={{0,32},{1,225},{32,64},{33,1},{64,96},{65,33},{96,128},{97,65},{12... | collective-permute-start | bytes 589832 | tf_op jit(solution)/shard_map/ppermute | solution.py:38
  87.3 1.2 collective-permute-start.7
  88.7 1.3 collective-permute-done.8
  89.9 5.4 %collective-permute-start.9 = (bf16[48,2048]{1,0:T(8,128)(2,1)S(1)}, bf16[48,2048]{1,0:T(8,128)(2,1)S(1)}, u32[]{:S(2)}, u32[]{:S(2)}) collective-permute-start(bf16[48,2048]{1,0:T(8,128)(2,1)S(1)} %collective-permute-done.8), channel_id=1, source_target_pairs={{0,1},{1,0},{2,3},{3,2},{4,5},{5,4},{6,7},{7,6},{8,9},{9,8},{10,11... | collective-permute-start | bytes 589832 | tf_op jit(solution)/shard_map/ppermute | solution.py:28
  95.4 1.0 collective-permute-done.9
  96.5 1.2 fusion.12
  97.7 1.2 fusion.8
  99.0 0.9 convolution_reduce_fusion
  100.4 1.4 multiply_reduce_fusion.1
  101.8 1.0 convolution_convert_fusion
  103.0 1.1 fusion.10
  104.1 1.2 add_convert_fusion
  107.6 5.7 %collective-permute-done.20 = bf16[48,2048]{1,0:T(8,128)(2,1)S(1)} collective-permute-done((bf16[48,2048]{1,0:T(8,128)(2,1)S(1)}, bf16[48,2048]{1,0:T(8,128)(2,1)S(1)}, u32[]{:S(2)}, u32[]{:S(2)}) %collective-permute-start.20) | collective-permute-done | bytes 196640 | tf_op jit(solution)/shard_map/ppermute | solution.py:38
  113.9 5.6 %collective-permute-done.11 = bf16[48,2048]{1,0:T(8,128)(2,1)S(1)} collective-permute-done((bf16[48,2048]{1,0:T(8,128)(2,1)S(1)}, bf16[48,2048]{1,0:T(8,128)(2,1)S(1)}, u32[]{:S(2)}, u32[]{:S(2)}) %collective-permute-start.11) | collective-permute-done | bytes 196640 | tf_op jit(solution)/shard_map/ppermute | solution.py:38
  120.1 1.1 collective-permute-start.13
  121.2 6.6 %collective-permute-done.22 = bf16[48,4096]{1,0:T(8,128)(2,1)S(1)} collective-permute-done((bf16[48,4096]{1,0:T(8,128)(2,1)S(1)}, bf16[48,4096]{1,0:T(8,128)(2,1)S(1)}, u32[]{:S(2)}, u32[]{:S(2)}) %collective-permute-start.22) | collective-permute-done | bytes 393248 | tf_op jit(solution)/shard_map/ppermute | solution.py:38
  128.0 4.0 %collective-permute-done.13 = bf16[48,4096]{1,0:T(8,128)(2,1)S(1)} collective-permute-done((bf16[48,4096]{1,0:T(8,128)(2,1)S(1)}, bf16[48,4096]{1,0:T(8,128)(2,1)S(1)}, u32[]{:S(2)}, u32[]{:S(2)}) %collective-permute-start.13) | collective-permute-done | bytes 393248 | tf_op jit(solution)/shard_map/ppermute | solution.py:38
  132.2 4.0 %collective-permute-done.24 = bf16[48,4096]{1,0:T(8,128)(2,1)S(1)} collective-permute-done((bf16[48,4096]{1,0:T(8,128)(2,1)S(1)}, bf16[48,4096]{1,0:T(8,128)(2,1)S(1)}, u32[]{:S(2)}, u32[]{:S(2)}) %collective-permute-start.24) | collective-permute-done | bytes 393248 | tf_op jit(solution)/shard_map/ppermute | solution.py:38
  136.4 4.0 %collective-permute-done.15 = bf16[48,4096]{1,0:T(8,128)(2,1)S(1)} collective-permute-done((bf16[48,4096]{1,0:T(8,128)(2,1)S(1)}, bf16[48,4096]{1,0:T(8,128)(2,1)S(1)}, u32[]{:S(2)}, u32[]{:S(2)}) %collective-permute-start.15) | collective-permute-done | bytes 393248 | tf_op jit(solution)/shard_map/ppermute | solution.py:38
  140.6 4.0 %collective-permute-done.26 = bf16[48,4096]{1,0:T(8,128)(2,1)S(1)} collective-permute-done((bf16[48,4096]{1,0:T(8,128)(2,1)S(1)}, bf16[48,4096]{1,0:T(8,128)(2,1)S(1)}, u32[]{:S(2)}, u32[]{:S(2)}) %collective-permute-start.26) | collective-permute-done | bytes 393248 | tf_op jit(solution)/shard_map/ppermute | solution.py:38
  144.7 1.2 collective-permute-start.27
  145.9 2.9 %collective-permute-done.17 = bf16[48,4096]{1,0:T(8,128)(2,1)S(1)} collective-permute-done((bf16[48,4096]{1,0:T(8,128)(2,1)S(1)}, bf16[48,4096]{1,0:T(8,128)(2,1)S(1)}, u32[]{:S(2)}, u32[]{:S(2)}) %collective-permute-start.17) | collective-permute-done | bytes 393248 | tf_op jit(solution)/shard_map/ppermute | solution.py:38
  148.9 1.2 collective-permute-start.18
  150.4 1.1 collective-permute-done.18
  151.9 0.9 copy.41
  152.8 6.5 %all-to-all-start.2 = ((bf16[16,112,128]{2,1,0:T(8,128)(2,1)}), bf16[16,112,128]{2,1,0:T(8,128)(2,1)S(1)}, u32[]{:S(2)}, u32[]{:S(2)}) async-start(bf16[16,112,128]{2,1,0:T(8,128)(2,1)} %copy.41), calls=%async_computation.2 | async-start | bytes 917504 | tf_op jit(solution)/shard_map/all_to_all | solution.py:42
  159.5 9.7 %all-to-all-done.2 = bf16[16,112,128]{2,1,0:T(8,128)(2,1)S(1)} async-done(((bf16[16,112,128]{2,1,0:T(8,128)(2,1)}), bf16[16,112,128]{2,1,0:T(8,128)(2,1)S(1)}, u32[]{:S(2)}, u32[]{:S(2)}) %all-to-all-start.2) | async-done | bytes 458784 | tf_op jit(solution)/shard_map/all_to_all | solution.py:42
  169.6 1.1 fusion.17
  170.6 1.1 fusion.18
  171.9 19.1 %all_to_all.20 = bf16[16,256,128]{2,1,0:T(8,128)(2,1)} all-to-all(bf16[16,256,128]{2,1,0:T(8,128)(2,1)S(1)} %broadcast_in_dim.16), channel_id=1, replica_groups=mesh['dp'=8,'y'=4,'xh'=2,'half'=2,'group'=2] {'y','xh','half'}, dimensions={0} | all-to-all | bytes 2097152 | tf_op jit(solution)/shard_map/all_to_all | solution.py:42
  191.0 1.5 copy.42
  192.5 2.8 %collective-permute-start.28 = (bf16[16,256,128]{1,2,0:T(8,128)(2,1)S(1)}, bf16[16,256,128]{1,2,0:T(8,128)(2,1)S(1)}, u32[]{:S(2)}, u32[]{:S(2)}) collective-permute-start(bf16[16,256,128]{1,2,0:T(8,128)(2,1)S(1)} %copy.42), channel_id=1, source_target_pairs={{0,1},{1,0},{2,3},{3,2},{4,5},{5,4},{6,7},{7,6},{8,9},{9,8},{10,11... | collective-permute-start | bytes 3145736 | tf_op jit(solution)/shard_map/ppermute | solution.py:28
  195.3 4.3 %fusion = bf16[1,224,4096]{2,1,0:T(8,128)(2,1)} fusion(bf16[384,224]{0,1:T(8,128)(2,1)S(1)} %get-tuple-element.18, bf16[384,4096]{1,0:T(8,128)(2,1)} %copy-done.1, f32[384]{0:T(512)S(1)} %add_divide_fusion.1), kind=kOutput, calls=%fused_computation.4 | convolution fusion | flops 710279168 | bytes 5154304 | tf_op jit(solution)/shard_map/dot_general | solution.py:12
  200.3 1.5 convolution_convert_fusion.5
  201.8 1.3 copy.44
  (110 shorter events, 9.1 us)
Async XLA Ops:
  7.2 4.6 %copy-start = (bf16[256,4096]{1,0:T(8,128)(2,1)S(1)}, bf16[256,4096]{1,0:T(8,128)(2,1)}, u32[]{:S(2)}) copy-start(bf16[256,4096]{1,0:T(8,128)(2,1)} %param.12) | copy-start | bytes 6291460
  7.2 53.3 %all-gather.3.cloned.1.call-start = ((), (), s32[]{:S(2)}) async-start(), calls=%async_computation.4 | async-start | bytes 3538944 | tf_op jit(solution)/shard_map/all_gather | solution.py:91
  13.9 5.1 %collective-permute-start = (bf16[128,2048]{1,0:T(8,128)(2,1)}, bf16[128,2048]{1,0:T(8,128)(2,1)}, u32[]{:S(2)}, u32[]{:S(2)}) collective-permute-start(bf16[128,2048]{1,0:T(8,128)(2,1)} %constant_dynamic-slice_fusion.4), channel_id=1, source_target_pairs={{0,1},{1,0},{2,3},{3,2},{4,5},{5,4},{6,7},{7,6},{8,9},{9,8},{10,11... | collective-permute-start | bytes 1572872 | tf_op jit(solution)/shard_map/ppermute | solution.py:28
  21.0 36.2 %copy-start.6 = (f32[4096]{0:T(1024)S(1)}, f32[4096]{0:T(1024)}, u32[]{:S(2)}) copy-start(f32[4096]{0:T(1024)} %param.13) | copy-start | bytes 49156
  21.0 15.9 %all-to-all-start = ((bf16[16,128,128]{2,1,0:T(8,128)(2,1)}), bf16[16,128,128]{2,1,0:T(8,128)(2,1)S(1)}, u32[]{:S(2)}, u32[]{:S(2)}) async-start(bf16[16,128,128]{2,1,0:T(8,128)(2,1)} %bitcast_bitcast_fusion), calls=%async_computation | async-start | bytes 1048576 | tf_op jit(solution)/shard_map/all_to_all | solution.py:42
  38.6 13.6 %all-to-all-start.1 = ((bf16[16,128,128]{2,1,0:T(8,128)(2,1)}), bf16[16,128,128]{2,1,0:T(8,128)(2,1)S(1)}, u32[]{:S(2)}, u32[]{:S(2)}) async-start(bf16[16,128,128]{2,1,0:T(8,128)(2,1)} %broadcast_in_dim.13), calls=%async_computation.1 | async-start | bytes 1048576 | tf_op jit(solution)/shard_map/all_to_all | solution.py:42
  52.5 4.1 %collective-permute-start.1 = (bf16[16,128,128]{1,2,0:T(8,128)(2,1)S(1)}, bf16[16,128,128]{1,2,0:T(8,128)(2,1)S(1)}, u32[]{:S(2)}, u32[]{:S(2)}) collective-permute-start(bf16[16,128,128]{1,2,0:T(8,128)(2,1)S(1)} %copy.39), channel_id=1, source_target_pairs={{0,1},{1,0},{2,3},{3,2},{4,5},{5,4},{6,7},{7,6},{8,9},{9,8},{10,11... | collective-permute-start | bytes 1572872 | tf_op jit(solution)/shard_map/ppermute | solution.py:28
  60.5 7.4 %copy-start.2 = (bf16[384,4096]{1,0:T(8,128)(2,1)S(1)}, bf16[384,4096]{1,0:T(8,128)(2,1)}, u32[]{:S(2)}) copy-start(bf16[384,4096]{1,0:T(8,128)(2,1)} %all-gather.3.cloned.1.call-done) | copy-start | bytes 9437188
  60.5 8.0 %collective-permute-start.2 = (bf16[48,4096]{1,0:T(8,128)(2,1)S(1)}, bf16[48,4096]{1,0:T(8,128)(2,1)S(1)}, u32[]{:S(2)}, u32[]{:S(2)}) collective-permute-start(bf16[48,4096]{1,0:T(8,128)(2,1)S(1)} %convolution_convert_fusion.3), channel_id=1, source_target_pairs={{0,32},{1,225},{32,64},{33,1},{64,96},{65,33},{96,128},{97,65},{12... | collective-permute-start | bytes 1179656 | tf_op jit(solution)/shard_map/ppermute | solution.py:38
  68.0 31.9 %copy-start.1 = (bf16[384,4096]{1,0:T(8,128)(2,1)}, bf16[384,4096]{1,0:T(8,128)(2,1)S(1)}, u32[]{:S(2)}) copy-start(bf16[384,4096]{1,0:T(8,128)(2,1)S(1)} %bitcast_dynamic-update-slice_fusion) | copy-start | bytes 9437188
  68.0 28.5 %copy-start.5 = (bf16[1,4096,224]{1,2,0:T(8,128)(2,1)S(1)}, bf16[1,4096,224]{1,2,0:T(8,128)(2,1)}, u32[]{:S(2)}) copy-start(bf16[1,4096,224]{1,2,0:T(8,128)(2,1)} %param.16) | copy-start | bytes 5505028
  68.4 7.8 %collective-permute-start.3 = (bf16[48,4096]{1,0:T(8,128)(2,1)S(1)}, bf16[48,4096]{1,0:T(8,128)(2,1)S(1)}, u32[]{:S(2)}, u32[]{:S(2)}) collective-permute-start(bf16[48,4096]{1,0:T(8,128)(2,1)S(1)} %collective-permute-done.2), channel_id=1, source_target_pairs={{0,32},{1,225},{32,64},{33,1},{64,96},{65,33},{96,128},{97,65},{12... | collective-permute-start | bytes 1179656 | tf_op jit(solution)/shard_map/ppermute | solution.py:38
  71.5 17.0 %collective-permute-start.5 = (bf16[48,4096]{1,0:T(8,128)(2,1)S(1)}, bf16[48,4096]{1,0:T(8,128)(2,1)S(1)}, u32[]{:S(2)}, u32[]{:S(2)}) collective-permute-start(bf16[48,4096]{1,0:T(8,128)(2,1)S(1)} %collective-permute-done.2), channel_id=1, source_target_pairs={{0,1},{1,0},{2,3},{3,2},{4,5},{5,4},{6,7},{7,6},{8,9},{9,8},{10,11... | collective-permute-start | bytes 1179656 | tf_op jit(solution)/shard_map/ppermute | solution.py:28
  76.3 7.8 %collective-permute-start.4 = (bf16[48,4096]{1,0:T(8,128)(2,1)S(1)}, bf16[48,4096]{1,0:T(8,128)(2,1)S(1)}, u32[]{:S(2)}, u32[]{:S(2)}) collective-permute-start(bf16[48,4096]{1,0:T(8,128)(2,1)S(1)} %collective-permute-done.3), channel_id=1, source_target_pairs={{0,32},{1,225},{32,64},{33,1},{64,96},{65,33},{96,128},{97,65},{12... | collective-permute-start | bytes 1179656 | tf_op jit(solution)/shard_map/ppermute | solution.py:38
  79.4 9.2 %collective-permute-start.6 = (bf16[48,4096]{1,0:T(8,128)(2,1)S(1)}, bf16[48,4096]{1,0:T(8,128)(2,1)S(1)}, u32[]{:S(2)}, u32[]{:S(2)}) collective-permute-start(bf16[48,4096]{1,0:T(8,128)(2,1)S(1)} %collective-permute-done.3), channel_id=1, source_target_pairs={{0,1},{1,0},{2,3},{3,2},{4,5},{5,4},{6,7},{7,6},{8,9},{9,8},{10,11... | collective-permute-start | bytes 1179656 | tf_op jit(solution)/shard_map/ppermute | solution.py:28
  84.1 5.8 %collective-permute-start.8 = (bf16[48,2048]{1,0:T(8,128)(2,1)S(1)}, bf16[48,2048]{1,0:T(8,128)(2,1)S(1)}, u32[]{:S(2)}, u32[]{:S(2)}) collective-permute-start(bf16[48,2048]{1,0:T(8,128)(2,1)S(1)} %constant_dynamic-slice_fusion.3), channel_id=1, source_target_pairs={{0,32},{1,225},{32,64},{33,1},{64,96},{65,33},{96,128},{97,65},{12... | collective-permute-start | bytes 589832 | tf_op jit(solution)/shard_map/ppermute | solution.py:38
  87.3 8.0 %collective-permute-start.7 = (bf16[48,4096]{1,0:T(8,128)(2,1)S(1)}, bf16[48,4096]{1,0:T(8,128)(2,1)S(1)}, u32[]{:S(2)}, u32[]{:S(2)}) collective-permute-start(bf16[48,4096]{1,0:T(8,128)(2,1)S(1)} %collective-permute-done.4), channel_id=1, source_target_pairs={{0,1},{1,0},{2,3},{3,2},{4,5},{5,4},{6,7},{7,6},{8,9},{9,8},{10,11... | collective-permute-start | bytes 1179656 | tf_op jit(solution)/shard_map/ppermute | solution.py:28
  89.9 6.5 %collective-permute-start.9 = (bf16[48,2048]{1,0:T(8,128)(2,1)S(1)}, bf16[48,2048]{1,0:T(8,128)(2,1)S(1)}, u32[]{:S(2)}, u32[]{:S(2)}) collective-permute-start(bf16[48,2048]{1,0:T(8,128)(2,1)S(1)} %collective-permute-done.8), channel_id=1, source_target_pairs={{0,1},{1,0},{2,3},{3,2},{4,5},{5,4},{6,7},{7,6},{8,9},{9,8},{10,11... | collective-permute-start | bytes 589832 | tf_op jit(solution)/shard_map/ppermute | solution.py:28
  95.4 2.4 %copy-start.3 = (bf16[1,4096,224]{1,2,0:T(8,128)(2,1)S(1)}, bf16[1,4096,224]{1,2,0:T(8,128)(2,1)}, u32[]{:S(2)}) copy-start(bf16[1,4096,224]{1,2,0:T(8,128)(2,1)} %param.17) | copy-start | bytes 5505028
  98.9 1.5 copy-start.4
  105.5 1.6 collective-permute-start.19
  106.0 1.5 collective-permute-start.10
  106.2 13.6 %collective-permute-start.12 = (bf16[48,4096]{1,0:T(8,128)(2,1)S(1)}, bf16[48,4096]{1,0:T(8,128)(2,1)S(1)}, u32[]{:S(2)}, u32[]{:S(2)}) collective-permute-start(bf16[48,4096]{1,0:T(8,128)(2,1)S(1)} %get-tuple-element.24), channel_id=1, source_target_pairs={{0,1},{1,0},{2,3},{3,2},{4,5},{5,4},{6,7},{7,6},{8,9},{9,8},{10,11... | collective-permute-start | bytes 1179656 | tf_op jit(solution)/shard_map/ppermute | solution.py:28
  106.6 21.4 %collective-permute-start.14 = (bf16[48,4096]{1,0:T(8,128)(2,1)S(1)}, bf16[48,4096]{1,0:T(8,128)(2,1)S(1)}, u32[]{:S(2)}, u32[]{:S(2)}) collective-permute-start(bf16[48,4096]{1,0:T(8,128)(2,1)S(1)} %get-tuple-element.23), channel_id=1, source_target_pairs={{0,1},{1,0},{2,3},{3,2},{4,5},{5,4},{6,7},{7,6},{8,9},{9,8},{10,11... | collective-permute-start | bytes 1179656 | tf_op jit(solution)/shard_map/ppermute | solution.py:28
  106.7 29.7 %collective-permute-start.16 = (bf16[48,4096]{1,0:T(8,128)(2,1)S(1)}, bf16[48,4096]{1,0:T(8,128)(2,1)S(1)}, u32[]{:S(2)}, u32[]{:S(2)}) collective-permute-start(bf16[48,4096]{1,0:T(8,128)(2,1)S(1)} %get-tuple-element.22), channel_id=1, source_target_pairs={{0,1},{1,0},{2,3},{3,2},{4,5},{5,4},{6,7},{7,6},{8,9},{9,8},{10,11... | collective-permute-start | bytes 1179656 | tf_op jit(solution)/shard_map/ppermute | solution.py:28
  107.1 6.4 %collective-permute-start.21 = (bf16[48,4096]{1,0:T(8,128)(2,1)S(1)}, bf16[48,4096]{1,0:T(8,128)(2,1)S(1)}, u32[]{:S(2)}, u32[]{:S(2)}) collective-permute-start(bf16[48,4096]{1,0:T(8,128)(2,1)S(1)} %get-tuple-element.28), channel_id=1, source_target_pairs={{0,1},{1,0},{2,3},{3,2},{4,5},{5,4},{6,7},{7,6},{8,9},{9,8},{10,11... | collective-permute-start | bytes 1179656 | tf_op jit(solution)/shard_map/ppermute | solution.py:28
  107.5 5.8 %collective-permute-start.20 = (bf16[48,2048]{1,0:T(8,128)(2,1)S(1)}, bf16[48,2048]{1,0:T(8,128)(2,1)S(1)}, u32[]{:S(2)}, u32[]{:S(2)}) collective-permute-start(bf16[48,2048]{1,0:T(8,128)(2,1)S(1)} %add_convert_fusion.10), channel_id=1, source_target_pairs={{0,224},{1,33},{32,0},{33,65},{64,32},{65,97},{96,64},{97,129},{12... | collective-permute-start | bytes 589832 | tf_op jit(solution)/shard_map/ppermute | solution.py:38
  113.3 6.8 %collective-permute-start.23 = (bf16[48,4096]{1,0:T(8,128)(2,1)S(1)}, bf16[48,4096]{1,0:T(8,128)(2,1)S(1)}, u32[]{:S(2)}, u32[]{:S(2)}) collective-permute-start(bf16[48,4096]{1,0:T(8,128)(2,1)S(1)} %get-tuple-element.27), channel_id=1, source_target_pairs={{0,1},{1,0},{2,3},{3,2},{4,5},{5,4},{6,7},{7,6},{8,9},{9,8},{10,11... | collective-permute-start | bytes 1179656 | tf_op jit(solution)/shard_map/ppermute | solution.py:28
  113.5 6.0 %collective-permute-start.11 = (bf16[48,2048]{1,0:T(8,128)(2,1)S(1)}, bf16[48,2048]{1,0:T(8,128)(2,1)S(1)}, u32[]{:S(2)}, u32[]{:S(2)}) collective-permute-start(bf16[48,2048]{1,0:T(8,128)(2,1)S(1)} %add_convert_fusion.11), channel_id=1, source_target_pairs={{0,224},{1,33},{32,0},{33,65},{64,32},{65,97},{96,64},{97,129},{12... | collective-permute-start | bytes 589832 | tf_op jit(solution)/shard_map/ppermute | solution.py:38
  119.5 12.7 %collective-permute-start.25 = (bf16[48,4096]{1,0:T(8,128)(2,1)S(1)}, bf16[48,4096]{1,0:T(8,128)(2,1)S(1)}, u32[]{:S(2)}, u32[]{:S(2)}) collective-permute-start(bf16[48,4096]{1,0:T(8,128)(2,1)S(1)} %get-tuple-element.26), channel_id=1, source_target_pairs={{0,1},{1,0},{2,3},{3,2},{4,5},{5,4},{6,7},{7,6},{8,9},{9,8},{10,11... | collective-permute-start | bytes 1179656 | tf_op jit(solution)/shard_map/ppermute | solution.py:28
  119.8 7.9 %collective-permute-start.22 = (bf16[48,4096]{1,0:T(8,128)(2,1)S(1)}, bf16[48,4096]{1,0:T(8,128)(2,1)S(1)}, u32[]{:S(2)}, u32[]{:S(2)}) collective-permute-start(bf16[48,4096]{1,0:T(8,128)(2,1)S(1)} %add_convert_fusion.5), channel_id=1, source_target_pairs={{0,224},{1,33},{32,0},{33,65},{64,32},{65,97},{96,64},{97,129},{12... | collective-permute-start | bytes 1179656 | tf_op jit(solution)/shard_map/ppermute | solution.py:38
  120.1 11.9 %collective-permute-start.13 = (bf16[48,4096]{1,0:T(8,128)(2,1)S(1)}, bf16[48,4096]{1,0:T(8,128)(2,1)S(1)}, u32[]{:S(2)}, u32[]{:S(2)}) collective-permute-start(bf16[48,4096]{1,0:T(8,128)(2,1)S(1)} %add_convert_fusion.9), channel_id=1, source_target_pairs={{0,224},{1,33},{32,0},{33,65},{64,32},{65,97},{96,64},{97,129},{12... | collective-permute-start | bytes 1179656 | tf_op jit(solution)/shard_map/ppermute | solution.py:38
  127.9 8.3 %collective-permute-start.24 = (bf16[48,4096]{1,0:T(8,128)(2,1)S(1)}, bf16[48,4096]{1,0:T(8,128)(2,1)S(1)}, u32[]{:S(2)}, u32[]{:S(2)}) collective-permute-start(bf16[48,4096]{1,0:T(8,128)(2,1)S(1)} %add_convert_fusion.4), channel_id=1, source_target_pairs={{0,224},{1,33},{32,0},{33,65},{64,32},{65,97},{96,64},{97,129},{12... | collective-permute-start | bytes 1179656 | tf_op jit(solution)/shard_map/ppermute | solution.py:38
  132.1 8.3 %collective-permute-start.15 = (bf16[48,4096]{1,0:T(8,128)(2,1)S(1)}, bf16[48,4096]{1,0:T(8,128)(2,1)S(1)}, u32[]{:S(2)}, u32[]{:S(2)}) collective-permute-start(bf16[48,4096]{1,0:T(8,128)(2,1)S(1)} %add_convert_fusion.8), channel_id=1, source_target_pairs={{0,224},{1,33},{32,0},{33,65},{64,32},{65,97},{96,64},{97,129},{12... | collective-permute-start | bytes 1179656 | tf_op jit(solution)/shard_map/ppermute | solution.py:38
  136.3 8.3 %collective-permute-start.26 = (bf16[48,4096]{1,0:T(8,128)(2,1)S(1)}, bf16[48,4096]{1,0:T(8,128)(2,1)S(1)}, u32[]{:S(2)}, u32[]{:S(2)}) collective-permute-start(bf16[48,4096]{1,0:T(8,128)(2,1)S(1)} %add_convert_fusion.3), channel_id=1, source_target_pairs={{0,224},{1,33},{32,0},{33,65},{64,32},{65,97},{96,64},{97,129},{12... | collective-permute-start | bytes 1179656 | tf_op jit(solution)/shard_map/ppermute | solution.py:38
  140.6 8.3 %collective-permute-start.17 = (bf16[48,4096]{1,0:T(8,128)(2,1)S(1)}, bf16[48,4096]{1,0:T(8,128)(2,1)S(1)}, u32[]{:S(2)}, u32[]{:S(2)}) collective-permute-start(bf16[48,4096]{1,0:T(8,128)(2,1)S(1)} %add_convert_fusion.7), channel_id=1, source_target_pairs={{0,224},{1,33},{32,0},{33,65},{64,32},{65,97},{96,64},{97,129},{12... | collective-permute-start | bytes 1179656 | tf_op jit(solution)/shard_map/ppermute | solution.py:38
  144.7 5.4 %collective-permute-start.27 = (bf16[48,4096]{1,0:T(8,128)(2,1)S(1)}, bf16[48,4096]{1,0:T(8,128)(2,1)S(1)}, u32[]{:S(2)}, u32[]{:S(2)}) collective-permute-start(bf16[48,4096]{1,0:T(8,128)(2,1)S(1)} %add_convert_fusion.2), channel_id=1, source_target_pairs={{0,1},{1,0},{2,3},{3,2},{4,5},{5,4},{6,7},{7,6},{8,9},{9,8},{10,11... | collective-permute-start | bytes 1179656 | tf_op jit(solution)/shard_map/ppermute | solution.py:28
  148.9 2.5 %collective-permute-start.18 = (bf16[48,4096]{1,0:T(8,128)(2,1)S(1)}, bf16[48,4096]{1,0:T(8,128)(2,1)S(1)}, u32[]{:S(2)}, u32[]{:S(2)}) collective-permute-start(bf16[48,4096]{1,0:T(8,128)(2,1)S(1)} %add_convert_fusion.6), channel_id=1, source_target_pairs={{0,1},{1,0},{2,3},{3,2},{4,5},{5,4},{6,7},{7,6},{8,9},{9,8},{10,11... | collective-permute-start | bytes 1179656 | tf_op jit(solution)/shard_map/ppermute | solution.py:28
  152.8 16.5 %all-to-all-start.2 = ((bf16[16,112,128]{2,1,0:T(8,128)(2,1)}), bf16[16,112,128]{2,1,0:T(8,128)(2,1)S(1)}, u32[]{:S(2)}, u32[]{:S(2)}) async-start(bf16[16,112,128]{2,1,0:T(8,128)(2,1)} %copy.41), calls=%async_computation.2 | async-start | bytes 917504 | tf_op jit(solution)/shard_map/all_to_all | solution.py:42
  192.5 7.2 %collective-permute-start.28 = (bf16[16,256,128]{1,2,0:T(8,128)(2,1)S(1)}, bf16[16,256,128]{1,2,0:T(8,128)(2,1)S(1)}, u32[]{:S(2)}, u32[]{:S(2)}) collective-permute-start(bf16[16,256,128]{1,2,0:T(8,128)(2,1)S(1)} %copy.42), channel_id=1, source_target_pairs={{0,1},{1,0},{2,3},{3,2},{4,5},{5,4},{6,7},{7,6},{8,9},{9,8},{10,11... | collective-permute-start | bytes 3145736 | tf_op jit(solution)/shard_map/ppermute | solution.py:28
Sparse Core Ops, SparseCore 0:
  11.9 48.5 all-gather.2
where the time goes:
time: 211 us; the launch traced here: 210 us
  waiting for transfers between devices  85 us (40%)
  starting transfers between devices  49.8 us (24%)
  matrix products  20.5 us (10%)
  blocking collectives  19.1 us (9%)
  between operations  14.8 us (7%)
  local copies, waits for them, and re-layouts  12.8 us (6%)
  other arithmetic  7.95 us (4%)
    ppermute x12, waiting for transfers between devices, hop(): return lax.ppermute(value, ('dp', 'group'), pairs)  47.6 us
    all_to_all x3, waiting for transfers between devices, exchange(): return lax.all_to_all(blocks, CHIPS, 0, 0)  29.4 us
    ppermute x17, starting transfers between devices, swap_core(): return lax.ppermute(value, 'group', [(0, 1), (1, 0)])  20 us
    all_to_all x1, blocking collectives, exchange(): return lax.all_to_all(blocks, CHIPS, 0, 0)  19.1 us
    all_to_all x3, starting transfers between devices, exchange(): return lax.all_to_all(blocks, CHIPS, 0, 0)  15.3 us
    ppermute x12, starting transfers between devices, hop(): return lax.ppermute(value, ('dp', 'group'), pairs)  14.5 us
    unnamed x30, local copies, waits for them, and re-layouts  7.25 us
    dot_general x5, matrix products, contract_cols(): lax.dot_general(left, right, (((1,), (1,)), ((), ())), preferred_element_...  6.09 us
  transfers between devices with their start and end apart: 33, of which 20 were waited for; matrix products, arithmetic and copies ran while one was open for 9% of the time, Pallas kernels for 0%

commit v1 on v0

--- a/solution.py
+++ b/solution.py
@@ -1,6 +1,8 @@
 import jax
 import jax.numpy as jnp
 from jax import lax
+from jax.experimental import pallas as pl
+from jax.experimental.pallas import tpu as pltpu
 from jax.sharding import Mesh, PartitionSpec as P
 
 BF = jnp.bfloat16
@@ -55,6 +57,48 @@
     mine = jnp.transpose(got, (1, 0, 2)).reshape(rows, 16 * width)
     other = jnp.transpose(other, (1, 0, 2)).reshape(rows, 16 * width)
     return join_halves(core, mine, other)
+
+
+def finish_kernel(core_ref, mine_ref, other_ref, proj_ref, layer_ref, grad_ref, cot_ref, total_ref):
+    rows, width = layer_ref.shape
+    block = mine_ref.shape[2]
+    core = core_ref[0]
+    half = width // 2
+
+    def place(chip, carry):
+        for ref, number in ((mine_ref, core), (other_ref, 1 - core)):
+            start = pl.multiple_of(number * half + chip * block, block)
+            layer_ref[:, pl.ds(start, block)] = ref[chip, :rows]
+            cot_ref[:, pl.ds(start, block)] = ref[chip, rows:]
+        return carry
+
+    lax.fori_loop(0, 16, place, 0)
+    total_ref[...] = jnp.zeros_like(total_ref)
+
+    def multiply(part, carry):
+        columns = pl.ds(pl.multiple_of(part * 1024, 1024), 1024)
+        total_ref[...] += contract_cols(cot_ref[:, columns], proj_ref[:, columns])
+        return carry
+
+    lax.fori_loop(0, width // 1024, multiply, 0)
+    grad_ref[...] = total_ref[...].astype(BF)
+
+
+def finish(core, mine, other, out_proj):
+    rows = mine.shape[1] // 2
+    channels, width = out_proj.shape
+    vmem = pl.BlockSpec(memory_space=pltpu.VMEM)
+    return pl.pallas_call(
+        finish_kernel,
+        out_shape=(
+            jax.ShapeDtypeStruct((rows, width), BF),
+            jax.ShapeDtypeStruct((rows, channels), BF),
+        ),
+        in_specs=[pl.BlockSpec(memory_space=pltpu.SMEM), vmem, vmem, vmem],
+        out_specs=(vmem, vmem),
+        scratch_shapes=[pltpu.VMEM((rows, width), BF), pltpu.VMEM((rows, channels), F32)],
+        compiler_params=pltpu.CompilerParams(vmem_limit_bytes=32 * 1024 * 1024),
+    )(core.reshape(1), mine, other, out_proj)
 
 
 def on_device(
@@ -192,9 +236,9 @@
         + inv_rms * (normed_cot * gain_here)
         - inv_rms * inv_rms * hidden * (inner / width)
     ).astype(BF)
-    final = gather_features(core, jnp.concatenate((layer_here, cot_out), axis=0))
-    layer_out = final[:rows]
-    grad_mixer = contract_cols(final[rows:], out_proj).astype(BF)
+    joined = jnp.concatenate((layer_here, cot_out), axis=0)
+    got = exchange(jnp.broadcast_to(joined[None], (16, 2 * rows, block)))
+    layer_out, grad_mixer = finish(core, got, swap_core(got), out_proj)
     return (layer_out, grad_mixer, grad_down)
 
 

time: 211 us -> 206 us (0.976)
  local copies, waits for them, and re-layouts: 12.8 us -> 9.35 us
  Pallas kernels: 0 us -> 2.54 us
  matrix products: 20.5 us -> 18.2 us
    pallas_call x0 -> x1, Pallas kernels: none -> 2.54 us  [finish(): pl.pallas_call(finish_kernel, out_shape=(jax.ShapeDtypeStruct((rows, widt...]
    unnamed x30 -> x31, local copies, waits for them, and re-layouts: 7.25 us -> 5.41 us
    dot_general x5 -> x4, matrix products: 6.09 us -> 4.62 us  [contract_cols(): lax.dot_general(left, right, (((1,), (1,)), ((), ())), preferred_element_...]
  transfers between devices with their start and end apart: 33 -> 33, of which waited for: 20 -> 20; matrix products, arithmetic and copies ran while one was open for 9% -> 8% of each run, Pallas kernels for 0% -> 0%
where the time goes in v1:
time: 206 us; the launch traced here: 205 us
  waiting for transfers between devices  84.9 us (41%)
  starting transfers between devices  49.6 us (24%)
  blocking collectives  19.2 us (9%)
  matrix products  18.2 us (9%)
  between operations  14.8 us (7%)
  local copies, waits for them, and re-layouts  9.35 us (5%)
  other arithmetic  6.39 us (3%)
  Pallas kernels  2.54 us (1%)
    ppermute x12, waiting for transfers between devices, hop(): return lax.ppermute(value, ('dp', 'group'), pairs)  47.2 us
    all_to_all x3, waiting for transfers between devices, exchange(): return lax.all_to_all(blocks, CHIPS, 0, 0)  29.4 us
    ppermute x17, starting transfers between devices, swap_core(): return lax.ppermute(value, 'group', [(0, 1), (1, 0)])  20.6 us
    all_to_all x1, blocking collectives, exchange(): return lax.all_to_all(blocks, CHIPS, 0, 0)  19.2 us
    all_to_all x3, starting transfers between devices, exchange(): return lax.all_to_all(blocks, CHIPS, 0, 0)  15.2 us
    ppermute x12, starting transfers between devices, hop(): return lax.ppermute(value, ('dp', 'group'), pairs)  13.8 us
    ppermute x17, waiting for transfers between devices, swap_core(): return lax.ppermute(value, 'group', [(0, 1), (1, 0)])  5.42 us
    unnamed x31, local copies, waits for them, and re-layouts  5.41 us
  transfers between devices with their start and end apart: 33, of which 20 were waited for; matrix products, arithmetic and copies ran while one was open for 8% of the time, Pallas kernels for 0%

profile of v1, /device:TPU:1, one launch (start us, length us, event | category | flops | bytes accessed | tf_op | source)
XLA Modules:
  0.0 204.9 jit_solution(16539537768680371804)
XLA Ops:
  7.2 0.9 copy.33
  8.7 0.7 multiply_add_fusion.1
  9.4 2.3 %convolution_convert_fusion.4 = bf16[48,4096]{1,0:T(8,128)(2,1)} fusion(bf16[128,4096]{1,0:T(8,128)(2,1)} %param.19, s32[128]{0:T(128)S(1)} %get-tuple-element.34, s32[128]{0:T(128)S(1)} %get-tuple-element.33, s32[48]{0:T(128)S(1)} %iota_add_fusion), kind=kOutput, calls=%fused_computation.7 | convolution fusion | flops 50546688 | bytes 1443008 | tf_op jit(solution)/shard_map/dot_general | solution.py:133
  11.8 2.1 %convolution_convert_fusion.2 = bf16[128,4096]{1,0:T(8,128)(2,1)S(1)} fusion(bf16[128,256]{1,0:T(8,128)(2,1)} %param.11, bf16[256,4096]{1,0:T(8,128)(2,1)} %proj_ref.1), kind=kOutput, calls=%fused_computation.5 | convolution fusion | flops 268959744 | bytes 3211264 | tf_op jit(solution)/shard_map/dot_general | solution.py:136
  13.8 0.8 constant_dynamic-slice_fusion.4
  14.7 3.2 %collective-permute-start = (bf16[128,2048]{1,0:T(8,128)(2,1)}, bf16[128,2048]{1,0:T(8,128)(2,1)S(1)}, u32[]{:S(2)}, u32[]{:S(2)}) collective-permute-start(bf16[128,2048]{1,0:T(8,128)(2,1)} %constant_dynamic-slice_fusion.4), channel_id=1, source_target_pairs={{0,1},{1,0},{2,3},{3,2},{4,5},{5,4},{6,7},{7,6},{8,9},{9,8},{10,11... | collective-permute-start | bytes 1572872 | tf_op jit(solution)/shard_map/ppermute | solution.py:30
  17.9 1.7 collective-permute-done
  19.7 1.0 bitcast_bitcast_fusion
  20.6 5.2 %all-to-all-start = ((bf16[16,128,128]{2,1,0:T(8,128)(2,1)}), bf16[16,128,128]{2,1,0:T(8,128)(2,1)S(1)}, u32[]{:S(2)}, u32[]{:S(2)}) async-start(bf16[16,128,128]{2,1,0:T(8,128)(2,1)} %bitcast_bitcast_fusion), calls=%async_computation | async-start | bytes 1048576 | tf_op jit(solution)/shard_map/all_to_all | solution.py:44
  25.8 10.7 %all-to-all-done = bf16[16,128,128]{2,1,0:T(8,128)(2,1)S(1)} async-done(((bf16[16,128,128]{2,1,0:T(8,128)(2,1)}), bf16[16,128,128]{2,1,0:T(8,128)(2,1)S(1)}, u32[]{:S(2)}, u32[]{:S(2)}) %all-to-all-start) | async-done | bytes 524320 | tf_op jit(solution)/shard_map/all_to_all | solution.py:44
  36.6 0.8 fusion.35
  37.3 0.9 broadcast_in_dim.13
  38.2 3.6 %all-to-all-start.1 = ((bf16[16,128,128]{2,1,0:T(8,128)(2,1)}), bf16[16,128,128]{2,1,0:T(8,128)(2,1)S(1)}, u32[]{:S(2)}, u32[]{:S(2)}) async-start(bf16[16,128,128]{2,1,0:T(8,128)(2,1)} %broadcast_in_dim.13), calls=%async_computation.1 | async-start | bytes 1048576 | tf_op jit(solution)/shard_map/all_to_all | solution.py:44
  41.9 0.9 reduce-precision_convert_fusion.1
  42.9 9.0 %all-to-all-done.1 = bf16[16,128,128]{2,1,0:T(8,128)(2,1)S(1)} async-done(((bf16[16,128,128]{2,1,0:T(8,128)(2,1)}), bf16[16,128,128]{2,1,0:T(8,128)(2,1)S(1)}, u32[]{:S(2)}, u32[]{:S(2)}) %all-to-all-start.1) | async-done | bytes 524320 | tf_op jit(solution)/shard_map/all_to_all | solution.py:44
  52.1 2.6 %collective-permute-start.1 = (bf16[16,128,128]{1,2,0:T(8,128)(2,1)S(1)}, bf16[16,128,128]{1,2,0:T(8,128)(2,1)S(1)}, u32[]{:S(2)}, u32[]{:S(2)}) collective-permute-start(bf16[16,128,128]{1,2,0:T(8,128)(2,1)S(1)} %copy.36), channel_id=1, source_target_pairs={{0,1},{1,0},{2,3},{3,2},{4,5},{5,4},{6,7},{7,6},{8,9},{9,8},{10,11... | collective-permute-start | bytes 1572872 | tf_op jit(solution)/shard_map/ppermute | solution.py:30
  54.8 1.5 collective-permute-done.1
  56.3 0.6 fusion.1
  56.8 0.8 convolution_convert_fusion.3
  57.6 2.8 %all-gather.3.cloned.1.call-done = bf16[384,4096]{1,0:T(8,128)(2,1)} async-done(((bf16[48,4096]{1,0:T(8,128)(2,1)}), bf16[384,4096]{1,0:T(8,128)(2,1)}) %all-gather.3.cloned.1.call-update) | async-done | bytes 3145744 | tf_op jit(solution)/shard_map/all_gather | solution.py:135
  60.5 2.9 %collective-permute-start.2 = (bf16[48,4096]{1,0:T(8,128)(2,1)S(1)}, bf16[48,4096]{1,0:T(8,128)(2,1)S(1)}, u32[]{:S(2)}, u32[]{:S(2)}) collective-permute-start(bf16[48,4096]{1,0:T(8,128)(2,1)S(1)} %convolution_convert_fusion.3), channel_id=1, source_target_pairs={{0,32},{1,225},{32,64},{33,1},{64,96},{65,33},{96,128},{97,65},{12... | collective-permute-start | bytes 1179656 | tf_op jit(solution)/shard_map/ppermute | solution.py:40
  63.3 1.0 bitcast_dynamic-update-slice_fusion.7
  64.4 1.0 bitcast_dynamic-update-slice_fusion.6
  65.4 1.0 bitcast_dynamic-update-slice_fusion.5
  66.4 1.0 bitcast_dynamic-update-slice_fusion.4
  67.7 0.4 collective-permute-done.2
  68.0 3.1 %collective-permute-start.3 = (bf16[48,4096]{1,0:T(8,128)(2,1)S(1)}, bf16[48,4096]{1,0:T(8,128)(2,1)S(1)}, u32[]{:S(2)}, u32[]{:S(2)}) collective-permute-start(bf16[48,4096]{1,0:T(8,128)(2,1)S(1)} %collective-permute-done.2), channel_id=1, source_target_pairs={{0,32},{1,225},{32,64},{33,1},{64,96},{65,33},{96,128},{97,65},{12... | collective-permute-start | bytes 1179656 | tf_op jit(solution)/shard_map/ppermute | solution.py:40
  71.2 4.7 %collective-permute-done.3 = bf16[48,4096]{1,0:T(8,128)(2,1)S(1)} collective-permute-done((bf16[48,4096]{1,0:T(8,128)(2,1)S(1)}, bf16[48,4096]{1,0:T(8,128)(2,1)S(1)}, u32[]{:S(2)}, u32[]{:S(2)}) %collective-permute-start.3) | collective-permute-done | bytes 393248 | tf_op jit(solution)/shard_map/ppermute | solution.py:40
  75.9 3.1 %collective-permute-start.4 = (bf16[48,4096]{1,0:T(8,128)(2,1)S(1)}, bf16[48,4096]{1,0:T(8,128)(2,1)S(1)}, u32[]{:S(2)}, u32[]{:S(2)}) collective-permute-start(bf16[48,4096]{1,0:T(8,128)(2,1)S(1)} %collective-permute-done.3), channel_id=1, source_target_pairs={{0,32},{1,225},{32,64},{33,1},{64,96},{65,33},{96,128},{97,65},{12... | collective-permute-start | bytes 1179656 | tf_op jit(solution)/shard_map/ppermute | solution.py:40
  79.4 4.3 %collective-permute-done.4 = bf16[48,4096]{1,0:T(8,128)(2,1)S(1)} collective-permute-done((bf16[48,4096]{1,0:T(8,128)(2,1)S(1)}, bf16[48,4096]{1,0:T(8,128)(2,1)S(1)}, u32[]{:S(2)}, u32[]{:S(2)}) %collective-permute-start.4) | collective-permute-done | bytes 393248 | tf_op jit(solution)/shard_map/ppermute | solution.py:40
  83.7 3.2 %collective-permute-start.8 = (bf16[48,2048]{1,0:T(8,128)(2,1)S(1)}, bf16[48,2048]{1,0:T(8,128)(2,1)S(1)}, u32[]{:S(2)}, u32[]{:S(2)}) collective-permute-start(bf16[48,2048]{1,0:T(8,128)(2,1)S(1)} %constant_dynamic-slice_fusion.3), channel_id=1, source_target_pairs={{0,32},{1,225},{32,64},{33,1},{64,96},{65,33},{96,128},{97,65},{12... | collective-permute-start | bytes 589832 | tf_op jit(solution)/shard_map/ppermute | solution.py:40
  86.9 1.6 collective-permute-start.7
  88.7 0.9 collective-permute-done.8
  89.6 5.8 %collective-permute-start.9 = (bf16[48,2048]{1,0:T(8,128)(2,1)S(1)}, bf16[48,2048]{1,0:T(8,128)(2,1)S(1)}, u32[]{:S(2)}, u32[]{:S(2)}) collective-permute-start(bf16[48,2048]{1,0:T(8,128)(2,1)S(1)} %collective-permute-done.8), channel_id=1, source_target_pairs={{0,1},{1,0},{2,3},{3,2},{4,5},{5,4},{6,7},{7,6},{8,9},{9,8},{10,11... | collective-permute-start | bytes 589832 | tf_op jit(solution)/shard_map/ppermute | solution.py:30
  95.4 1.0 collective-permute-done.9
  96.5 1.2 fusion.12
  97.7 1.2 fusion.8
  98.9 0.9 convolution_reduce_fusion
  99.9 1.3 multiply_reduce_fusion.1
  101.2 1.0 convolution_convert_fusion
  102.4 1.1 fusion.10
  103.5 1.3 add_convert_fusion
  105.0 0.4 collective-permute-start.19
  107.1 5.7 %collective-permute-done.20 = bf16[48,2048]{1,0:T(8,128)(2,1)S(1)} collective-permute-done((bf16[48,2048]{1,0:T(8,128)(2,1)S(1)}, bf16[48,2048]{1,0:T(8,128)(2,1)S(1)}, u32[]{:S(2)}, u32[]{:S(2)}) %collective-permute-start.20) | collective-permute-done | bytes 196640 | tf_op jit(solution)/shard_map/ppermute | solution.py:40
  113.4 5.6 %collective-permute-done.11 = bf16[48,2048]{1,0:T(8,128)(2,1)S(1)} collective-permute-done((bf16[48,2048]{1,0:T(8,128)(2,1)S(1)}, bf16[48,2048]{1,0:T(8,128)(2,1)S(1)}, u32[]{:S(2)}, u32[]{:S(2)}) %collective-permute-start.11) | collective-permute-done | bytes 196640 | tf_op jit(solution)/shard_map/ppermute | solution.py:40
  119.5 0.7 collective-permute-start.13
  120.2 6.9 %collective-permute-done.22 = bf16[48,4096]{1,0:T(8,128)(2,1)S(1)} collective-permute-done((bf16[48,4096]{1,0:T(8,128)(2,1)S(1)}, bf16[48,4096]{1,0:T(8,128)(2,1)S(1)}, u32[]{:S(2)}, u32[]{:S(2)}) %collective-permute-start.22) | collective-permute-done | bytes 393248 | tf_op jit(solution)/shard_map/ppermute | solution.py:40
  127.4 4.0 %collective-permute-done.13 = bf16[48,4096]{1,0:T(8,128)(2,1)S(1)} collective-permute-done((bf16[48,4096]{1,0:T(8,128)(2,1)S(1)}, bf16[48,4096]{1,0:T(8,128)(2,1)S(1)}, u32[]{:S(2)}, u32[]{:S(2)}) %collective-permute-start.13) | collective-permute-done | bytes 393248 | tf_op jit(solution)/shard_map/ppermute | solution.py:40
  131.7 4.0 %collective-permute-done.24 = bf16[48,4096]{1,0:T(8,128)(2,1)S(1)} collective-permute-done((bf16[48,4096]{1,0:T(8,128)(2,1)S(1)}, bf16[48,4096]{1,0:T(8,128)(2,1)S(1)}, u32[]{:S(2)}, u32[]{:S(2)}) %collective-permute-start.24) | collective-permute-done | bytes 393248 | tf_op jit(solution)/shard_map/ppermute | solution.py:40
  135.9 4.0 %collective-permute-done.15 = bf16[48,4096]{1,0:T(8,128)(2,1)S(1)} collective-permute-done((bf16[48,4096]{1,0:T(8,128)(2,1)S(1)}, bf16[48,4096]{1,0:T(8,128)(2,1)S(1)}, u32[]{:S(2)}, u32[]{:S(2)}) %collective-permute-start.15) | collective-permute-done | bytes 393248 | tf_op jit(solution)/shard_map/ppermute | solution.py:40
  140.1 4.0 %collective-permute-done.26 = bf16[48,4096]{1,0:T(8,128)(2,1)S(1)} collective-permute-done((bf16[48,4096]{1,0:T(8,128)(2,1)S(1)}, bf16[48,4096]{1,0:T(8,128)(2,1)S(1)}, u32[]{:S(2)}, u32[]{:S(2)}) %collective-permute-start.26) | collective-permute-done | bytes 393248 | tf_op jit(solution)/shard_map/ppermute | solution.py:40
  144.1 1.2 collective-permute-start.27
  145.3 2.9 %collective-permute-done.17 = bf16[48,4096]{1,0:T(8,128)(2,1)S(1)} collective-permute-done((bf16[48,4096]{1,0:T(8,128)(2,1)S(1)}, bf16[48,4096]{1,0:T(8,128)(2,1)S(1)}, u32[]{:S(2)}, u32[]{:S(2)}) %collective-permute-start.17) | collective-permute-done | bytes 393248 | tf_op jit(solution)/shard_map/ppermute | solution.py:40
  148.4 1.2 collective-permute-start.18
  149.8 1.1 collective-permute-done.18
  151.3 0.9 copy.38
  152.2 6.5 %all-to-all-start.2 = ((bf16[16,112,128]{2,1,0:T(8,128)(2,1)}), bf16[16,112,128]{2,1,0:T(8,128)(2,1)S(1)}, u32[]{:S(2)}, u32[]{:S(2)}) async-start(bf16[16,112,128]{2,1,0:T(8,128)(2,1)} %copy.38), calls=%async_computation.2 | async-start | bytes 917504 | tf_op jit(solution)/shard_map/all_to_all | solution.py:44
  158.9 9.7 %all-to-all-done.2 = bf16[16,112,128]{2,1,0:T(8,128)(2,1)S(1)} async-done(((bf16[16,112,128]{2,1,0:T(8,128)(2,1)}), bf16[16,112,128]{2,1,0:T(8,128)(2,1)S(1)}, u32[]{:S(2)}, u32[]{:S(2)}) %all-to-all-start.2) | async-done | bytes 458784 | tf_op jit(solution)/shard_map/all_to_all | solution.py:44
  169.0 1.2 fusion.17
  170.2 1.1 fusion.18
  171.5 19.2 %all_to_all.20.mine_ref = bf16[16,256,128]{2,1,0:T(8,128)(2,1)S(1)} all-to-all(bf16[16,256,128]{2,1,0:T(8,128)(2,1)S(1)} %broadcast_in_dim.16), channel_id=1, replica_groups=mesh['dp'=8,'y'=4,'xh'=2,'half'=2,'group'=2] {'y','xh','half'}, dimensions={0} | all-to-all | bytes 2097152 | tf_op jit(solution)/shard_map/all_to_all | solution.py:44
  190.7 2.4 %collective-permute-start.28 = (bf16[16,256,128]{2,1,0:T(8,128)(2,1)S(1)}, bf16[16,256,128]{2,1,0:T(8,128)(2,1)S(1)}, u32[]{:S(2)}, u32[]{:S(2)}) collective-permute-start(bf16[16,256,128]{2,1,0:T(8,128)(2,1)S(1)} %all_to_all.20.mine_ref), channel_id=1, source_target_pairs={{0,1},{1,0},{2,3},{3,2},{4,5},{5,4},{6,7},{7,6},{8,9},{9,8},{10,11... | collective-permute-start | bytes 3145736 | tf_op jit(solution)/shard_map/ppermute | solution.py:30
  193.1 2.5 %fusion = bf16[1,224,4096]{2,1,0:T(8,128)(2,1)} fusion(bf16[384,224]{0,1:T(8,128)(2,1)S(1)} %get-tuple-element.16, bf16[384,4096]{1,0:T(8,128)(2,1)S(1)} %copy-done.3, f32[384]{0:T(512)S(1)} %add_divide_fusion.1), kind=kOutput, calls=%fused_computation.4 | convolution fusion | flops 710279168 | bytes 5154304 | tf_op jit(solution)/shard_map/dot_general | solution.py:14
  195.5 2.5 %shard_map.121 = (bf16[128,4096]{1,0:T(8,128)(2,1)}, bf16[128,256]{1,0:T(8,128)(2,1)}) custom-call(s32[1]{0:T(128)} %bitcast.core_ref, bf16[16,256,128]{2,1,0:T(8,128)(2,1)S(1)} %all_to_all.20.mine_ref, bf16[16,256,128]{2,1,0:T(8,128)(2,1)S(1)} %collective-permute-done.28.other_ref, bf16[256,4096]{1,0:T(8,128)(2,1)S(1)} %copy-done.1), custom_call_target="tpu_custom_call" | custom-call | tf_op jit(solution)/shard_map/pallas_call | solution.py:91
  (108 shorter events, 7.5 us)
Async XLA Ops:
  7.2 92.8 %copy-start = (bf16[1,224,4096]{2,1,0:T(8,128)(2,1)S(1)}, bf16[1,224,4096]{2,1,0:T(8,128)(2,1)}, u32[]{:S(2)}) copy-start(bf16[1,224,4096]{2,1,0:T(8,128)(2,1)} %param.18) | copy-start | bytes 5505028
  7.2 53.3 %all-gather.3.cloned.1.call-start = ((), (), s32[]{:S(2)}) async-start(), calls=%async_computation.4 | async-start | bytes 3538944 | tf_op jit(solution)/shard_map/all_gather | solution.py:135
  14.7 5.0 %collective-permute-start = (bf16[128,2048]{1,0:T(8,128)(2,1)}, bf16[128,2048]{1,0:T(8,128)(2,1)S(1)}, u32[]{:S(2)}, u32[]{:S(2)}) collective-permute-start(bf16[128,2048]{1,0:T(8,128)(2,1)} %constant_dynamic-slice_fusion.4), channel_id=1, source_target_pairs={{0,1},{1,0},{2,3},{3,2},{4,5},{5,4},{6,7},{7,6},{8,9},{9,8},{10,11... | collective-permute-start | bytes 1572872 | tf_op jit(solution)/shard_map/ppermute | solution.py:30
  20.6 36.2 %copy-start.7 = (f32[4096]{0:T(1024)S(1)}, f32[4096]{0:T(1024)}, u32[]{:S(2)}) copy-start(f32[4096]{0:T(1024)} %param.13) | copy-start | bytes 49156
  20.6 15.9 %all-to-all-start = ((bf16[16,128,128]{2,1,0:T(8,128)(2,1)}), bf16[16,128,128]{2,1,0:T(8,128)(2,1)S(1)}, u32[]{:S(2)}, u32[]{:S(2)}) async-start(bf16[16,128,128]{2,1,0:T(8,128)(2,1)} %bitcast_bitcast_fusion), calls=%async_computation | async-start | bytes 1048576 | tf_op jit(solution)/shard_map/all_to_all | solution.py:44
  38.2 13.6 %all-to-all-start.1 = ((bf16[16,128,128]{2,1,0:T(8,128)(2,1)}), bf16[16,128,128]{2,1,0:T(8,128)(2,1)S(1)}, u32[]{:S(2)}, u32[]{:S(2)}) async-start(bf16[16,128,128]{2,1,0:T(8,128)(2,1)} %broadcast_in_dim.13), calls=%async_computation.1 | async-start | bytes 1048576 | tf_op jit(solution)/shard_map/all_to_all | solution.py:44
  52.1 4.1 %collective-permute-start.1 = (bf16[16,128,128]{1,2,0:T(8,128)(2,1)S(1)}, bf16[16,128,128]{1,2,0:T(8,128)(2,1)S(1)}, u32[]{:S(2)}, u32[]{:S(2)}) collective-permute-start(bf16[16,128,128]{1,2,0:T(8,128)(2,1)S(1)} %copy.36), channel_id=1, source_target_pairs={{0,1},{1,0},{2,3},{3,2},{4,5},{5,4},{6,7},{7,6},{8,9},{9,8},{10,11... | collective-permute-start | bytes 1572872 | tf_op jit(solution)/shard_map/ppermute | solution.py:30
  60.5 7.0 %copy-start.4 = (bf16[384,4096]{1,0:T(8,128)(2,1)S(1)}, bf16[384,4096]{1,0:T(8,128)(2,1)}, u32[]{:S(2)}) copy-start(bf16[384,4096]{1,0:T(8,128)(2,1)} %all-gather.3.cloned.1.call-done) | copy-start | bytes 9437188
  60.5 7.6 %collective-permute-start.2 = (bf16[48,4096]{1,0:T(8,128)(2,1)S(1)}, bf16[48,4096]{1,0:T(8,128)(2,1)S(1)}, u32[]{:S(2)}, u32[]{:S(2)}) collective-permute-start(bf16[48,4096]{1,0:T(8,128)(2,1)S(1)} %convolution_convert_fusion.3), channel_id=1, source_target_pairs={{0,32},{1,225},{32,64},{33,1},{64,96},{65,33},{96,128},{97,65},{12... | collective-permute-start | bytes 1179656 | tf_op jit(solution)/shard_map/ppermute | solution.py:40
  67.6 32.3 %copy-start.2 = (bf16[384,4096]{1,0:T(8,128)(2,1)}, bf16[384,4096]{1,0:T(8,128)(2,1)S(1)}, u32[]{:S(2)}) copy-start(bf16[384,4096]{1,0:T(8,128)(2,1)S(1)} %bitcast_dynamic-update-slice_fusion) | copy-start | bytes 9437188
  67.7 28.8 %copy-start.6 = (bf16[1,4096,224]{1,2,0:T(8,128)(2,1)S(1)}, bf16[1,4096,224]{1,2,0:T(8,128)(2,1)}, u32[]{:S(2)}) copy-start(bf16[1,4096,224]{1,2,0:T(8,128)(2,1)} %param.16) | copy-start | bytes 5505028
  68.0 7.8 %collective-permute-start.3 = (bf16[48,4096]{1,0:T(8,128)(2,1)S(1)}, bf16[48,4096]{1,0:T(8,128)(2,1)S(1)}, u32[]{:S(2)}, u32[]{:S(2)}) collective-permute-start(bf16[48,4096]{1,0:T(8,128)(2,1)S(1)} %collective-permute-done.2), channel_id=1, source_target_pairs={{0,32},{1,225},{32,64},{33,1},{64,96},{65,33},{96,128},{97,65},{12... | collective-permute-start | bytes 1179656 | tf_op jit(solution)/shard_map/ppermute | solution.py:40
  71.2 17.4 %collective-permute-start.5 = (bf16[48,4096]{1,0:T(8,128)(2,1)S(1)}, bf16[48,4096]{1,0:T(8,128)(2,1)S(1)}, u32[]{:S(2)}, u32[]{:S(2)}) collective-permute-start(bf16[48,4096]{1,0:T(8,128)(2,1)S(1)} %collective-permute-done.2), channel_id=1, source_target_pairs={{0,1},{1,0},{2,3},{3,2},{4,5},{5,4},{6,7},{7,6},{8,9},{9,8},{10,11... | collective-permute-start | bytes 1179656 | tf_op jit(solution)/shard_map/ppermute | solution.py:30
  75.9 7.8 %collective-permute-start.4 = (bf16[48,4096]{1,0:T(8,128)(2,1)S(1)}, bf16[48,4096]{1,0:T(8,128)(2,1)S(1)}, u32[]{:S(2)}, u32[]{:S(2)}) collective-permute-start(bf16[48,4096]{1,0:T(8,128)(2,1)S(1)} %collective-permute-done.3), channel_id=1, source_target_pairs={{0,32},{1,225},{32,64},{33,1},{64,96},{65,33},{96,128},{97,65},{12... | collective-permute-start | bytes 1179656 | tf_op jit(solution)/shard_map/ppermute | solution.py:40
  79.0 9.6 %collective-permute-start.6 = (bf16[48,4096]{1,0:T(8,128)(2,1)S(1)}, bf16[48,4096]{1,0:T(8,128)(2,1)S(1)}, u32[]{:S(2)}, u32[]{:S(2)}) collective-permute-start(bf16[48,4096]{1,0:T(8,128)(2,1)S(1)} %collective-permute-done.3), channel_id=1, source_target_pairs={{0,1},{1,0},{2,3},{3,2},{4,5},{5,4},{6,7},{7,6},{8,9},{9,8},{10,11... | collective-permute-start | bytes 1179656 | tf_op jit(solution)/shard_map/ppermute | solution.py:30
  83.7 5.8 %collective-permute-start.8 = (bf16[48,2048]{1,0:T(8,128)(2,1)S(1)}, bf16[48,2048]{1,0:T(8,128)(2,1)S(1)}, u32[]{:S(2)}, u32[]{:S(2)}) collective-permute-start(bf16[48,2048]{1,0:T(8,128)(2,1)S(1)} %constant_dynamic-slice_fusion.3), channel_id=1, source_target_pairs={{0,32},{1,225},{32,64},{33,1},{64,96},{65,33},{96,128},{97,65},{12... | collective-permute-start | bytes 589832 | tf_op jit(solution)/shard_map/ppermute | solution.py:40
  86.9 8.4 %collective-permute-start.7 = (bf16[48,4096]{1,0:T(8,128)(2,1)S(1)}, bf16[48,4096]{1,0:T(8,128)(2,1)S(1)}, u32[]{:S(2)}, u32[]{:S(2)}) collective-permute-start(bf16[48,4096]{1,0:T(8,128)(2,1)S(1)} %collective-permute-done.4), channel_id=1, source_target_pairs={{0,1},{1,0},{2,3},{3,2},{4,5},{5,4},{6,7},{7,6},{8,9},{9,8},{10,11... | collective-permute-start | bytes 1179656 | tf_op jit(solution)/shard_map/ppermute | solution.py:30
  89.6 6.8 %collective-permute-start.9 = (bf16[48,2048]{1,0:T(8,128)(2,1)S(1)}, bf16[48,2048]{1,0:T(8,128)(2,1)S(1)}, u32[]{:S(2)}, u32[]{:S(2)}) collective-permute-start(bf16[48,2048]{1,0:T(8,128)(2,1)S(1)} %collective-permute-done.8), channel_id=1, source_target_pairs={{0,1},{1,0},{2,3},{3,2},{4,5},{5,4},{6,7},{7,6},{8,9},{9,8},{10,11... | collective-permute-start | bytes 589832 | tf_op jit(solution)/shard_map/ppermute | solution.py:30
  95.3 2.4 %copy-start.5 = (bf16[1,4096,224]{1,2,0:T(8,128)(2,1)S(1)}, bf16[1,4096,224]{1,2,0:T(8,128)(2,1)}, u32[]{:S(2)}) copy-start(bf16[1,4096,224]{1,2,0:T(8,128)(2,1)} %param.17) | copy-start | bytes 5505028
  105.0 1.6 collective-permute-start.19
  105.4 1.5 collective-permute-start.10
  105.7 13.6 %collective-permute-start.12 = (bf16[48,4096]{1,0:T(8,128)(2,1)S(1)}, bf16[48,4096]{1,0:T(8,128)(2,1)S(1)}, u32[]{:S(2)}, u32[]{:S(2)}) collective-permute-start(bf16[48,4096]{1,0:T(8,128)(2,1)S(1)} %get-tuple-element.22), channel_id=1, source_target_pairs={{0,1},{1,0},{2,3},{3,2},{4,5},{5,4},{6,7},{7,6},{8,9},{9,8},{10,11... | collective-permute-start | bytes 1179656 | tf_op jit(solution)/shard_map/ppermute | solution.py:30
  106.0 21.4 %collective-permute-start.14 = (bf16[48,4096]{1,0:T(8,128)(2,1)S(1)}, bf16[48,4096]{1,0:T(8,128)(2,1)S(1)}, u32[]{:S(2)}, u32[]{:S(2)}) collective-permute-start(bf16[48,4096]{1,0:T(8,128)(2,1)S(1)} %get-tuple-element.21), channel_id=1, source_target_pairs={{0,1},{1,0},{2,3},{3,2},{4,5},{5,4},{6,7},{7,6},{8,9},{9,8},{10,11... | collective-permute-start | bytes 1179656 | tf_op jit(solution)/shard_map/ppermute | solution.py:30
  106.2 29.7 %collective-permute-start.16 = (bf16[48,4096]{1,0:T(8,128)(2,1)S(1)}, bf16[48,4096]{1,0:T(8,128)(2,1)S(1)}, u32[]{:S(2)}, u32[]{:S(2)}) collective-permute-start(bf16[48,4096]{1,0:T(8,128)(2,1)S(1)} %get-tuple-element.20), channel_id=1, source_target_pairs={{0,1},{1,0},{2,3},{3,2},{4,5},{5,4},{6,7},{7,6},{8,9},{9,8},{10,11... | collective-permute-start | bytes 1179656 | tf_op jit(solution)/shard_map/ppermute | solution.py:30
  106.5 6.4 %collective-permute-start.21 = (bf16[48,4096]{1,0:T(8,128)(2,1)S(1)}, bf16[48,4096]{1,0:T(8,128)(2,1)S(1)}, u32[]{:S(2)}, u32[]{:S(2)}) collective-permute-start(bf16[48,4096]{1,0:T(8,128)(2,1)S(1)} %get-tuple-element.26), channel_id=1, source_target_pairs={{0,1},{1,0},{2,3},{3,2},{4,5},{5,4},{6,7},{7,6},{8,9},{9,8},{10,11... | collective-permute-start | bytes 1179656 | tf_op jit(solution)/shard_map/ppermute | solution.py:30
  106.9 5.8 %collective-permute-start.20 = (bf16[48,2048]{1,0:T(8,128)(2,1)S(1)}, bf16[48,2048]{1,0:T(8,128)(2,1)S(1)}, u32[]{:S(2)}, u32[]{:S(2)}) collective-permute-start(bf16[48,2048]{1,0:T(8,128)(2,1)S(1)} %add_convert_fusion.10), channel_id=1, source_target_pairs={{0,224},{1,33},{32,0},{33,65},{64,32},{65,97},{96,64},{97,129},{12... | collective-permute-start | bytes 589832 | tf_op jit(solution)/shard_map/ppermute | solution.py:40
  112.7 6.8 %collective-permute-start.23 = (bf16[48,4096]{1,0:T(8,128)(2,1)S(1)}, bf16[48,4096]{1,0:T(8,128)(2,1)S(1)}, u32[]{:S(2)}, u32[]{:S(2)}) collective-permute-start(bf16[48,4096]{1,0:T(8,128)(2,1)S(1)} %get-tuple-element.25), channel_id=1, source_target_pairs={{0,1},{1,0},{2,3},{3,2},{4,5},{5,4},{6,7},{7,6},{8,9},{9,8},{10,11... | collective-permute-start | bytes 1179656 | tf_op jit(solution)/shard_map/ppermute | solution.py:30
  112.9 6.0 %collective-permute-start.11 = (bf16[48,2048]{1,0:T(8,128)(2,1)S(1)}, bf16[48,2048]{1,0:T(8,128)(2,1)S(1)}, u32[]{:S(2)}, u32[]{:S(2)}) collective-permute-start(bf16[48,2048]{1,0:T(8,128)(2,1)S(1)} %add_convert_fusion.11), channel_id=1, source_target_pairs={{0,224},{1,33},{32,0},{33,65},{64,32},{65,97},{96,64},{97,129},{12... | collective-permute-start | bytes 589832 | tf_op jit(solution)/shard_map/ppermute | solution.py:40
  118.9 12.7 %collective-permute-start.25 = (bf16[48,4096]{1,0:T(8,128)(2,1)S(1)}, bf16[48,4096]{1,0:T(8,128)(2,1)S(1)}, u32[]{:S(2)}, u32[]{:S(2)}) collective-permute-start(bf16[48,4096]{1,0:T(8,128)(2,1)S(1)} %get-tuple-element.24), channel_id=1, source_target_pairs={{0,1},{1,0},{2,3},{3,2},{4,5},{5,4},{6,7},{7,6},{8,9},{9,8},{10,11... | collective-permute-start | bytes 1179656 | tf_op jit(solution)/shard_map/ppermute | solution.py:30
  119.3 7.9 %collective-permute-start.22 = (bf16[48,4096]{1,0:T(8,128)(2,1)S(1)}, bf16[48,4096]{1,0:T(8,128)(2,1)S(1)}, u32[]{:S(2)}, u32[]{:S(2)}) collective-permute-start(bf16[48,4096]{1,0:T(8,128)(2,1)S(1)} %add_convert_fusion.5), channel_id=1, source_target_pairs={{0,224},{1,33},{32,0},{33,65},{64,32},{65,97},{96,64},{97,129},{12... | collective-permute-start | bytes 1179656 | tf_op jit(solution)/shard_map/ppermute | solution.py:40
  119.5 11.9 %collective-permute-start.13 = (bf16[48,4096]{1,0:T(8,128)(2,1)S(1)}, bf16[48,4096]{1,0:T(8,128)(2,1)S(1)}, u32[]{:S(2)}, u32[]{:S(2)}) collective-permute-start(bf16[48,4096]{1,0:T(8,128)(2,1)S(1)} %add_convert_fusion.9), channel_id=1, source_target_pairs={{0,224},{1,33},{32,0},{33,65},{64,32},{65,97},{96,64},{97,129},{12... | collective-permute-start | bytes 1179656 | tf_op jit(solution)/shard_map/ppermute | solution.py:40
  127.3 8.3 %collective-permute-start.24 = (bf16[48,4096]{1,0:T(8,128)(2,1)S(1)}, bf16[48,4096]{1,0:T(8,128)(2,1)S(1)}, u32[]{:S(2)}, u32[]{:S(2)}) collective-permute-start(bf16[48,4096]{1,0:T(8,128)(2,1)S(1)} %add_convert_fusion.4), channel_id=1, source_target_pairs={{0,224},{1,33},{32,0},{33,65},{64,32},{65,97},{96,64},{97,129},{12... | collective-permute-start | bytes 1179656 | tf_op jit(solution)/shard_map/ppermute | solution.py:40
  131.6 8.3 %collective-permute-start.15 = (bf16[48,4096]{1,0:T(8,128)(2,1)S(1)}, bf16[48,4096]{1,0:T(8,128)(2,1)S(1)}, u32[]{:S(2)}, u32[]{:S(2)}) collective-permute-start(bf16[48,4096]{1,0:T(8,128)(2,1)S(1)} %add_convert_fusion.8), channel_id=1, source_target_pairs={{0,224},{1,33},{32,0},{33,65},{64,32},{65,97},{96,64},{97,129},{12... | collective-permute-start | bytes 1179656 | tf_op jit(solution)/shard_map/ppermute | solution.py:40
  135.8 8.3 %collective-permute-start.26 = (bf16[48,4096]{1,0:T(8,128)(2,1)S(1)}, bf16[48,4096]{1,0:T(8,128)(2,1)S(1)}, u32[]{:S(2)}, u32[]{:S(2)}) collective-permute-start(bf16[48,4096]{1,0:T(8,128)(2,1)S(1)} %add_convert_fusion.3), channel_id=1, source_target_pairs={{0,224},{1,33},{32,0},{33,65},{64,32},{65,97},{96,64},{97,129},{12... | collective-permute-start | bytes 1179656 | tf_op jit(solution)/shard_map/ppermute | solution.py:40
  140.0 8.3 %collective-permute-start.17 = (bf16[48,4096]{1,0:T(8,128)(2,1)S(1)}, bf16[48,4096]{1,0:T(8,128)(2,1)S(1)}, u32[]{:S(2)}, u32[]{:S(2)}) collective-permute-start(bf16[48,4096]{1,0:T(8,128)(2,1)S(1)} %add_convert_fusion.7), channel_id=1, source_target_pairs={{0,224},{1,33},{32,0},{33,65},{64,32},{65,97},{96,64},{97,129},{12... | collective-permute-start | bytes 1179656 | tf_op jit(solution)/shard_map/ppermute | solution.py:40
  144.1 5.4 %collective-permute-start.27 = (bf16[48,4096]{1,0:T(8,128)(2,1)S(1)}, bf16[48,4096]{1,0:T(8,128)(2,1)S(1)}, u32[]{:S(2)}, u32[]{:S(2)}) collective-permute-start(bf16[48,4096]{1,0:T(8,128)(2,1)S(1)} %add_convert_fusion.2), channel_id=1, source_target_pairs={{0,1},{1,0},{2,3},{3,2},{4,5},{5,4},{6,7},{7,6},{8,9},{9,8},{10,11... | collective-permute-start | bytes 1179656 | tf_op jit(solution)/shard_map/ppermute | solution.py:30
  148.4 2.5 %collective-permute-start.18 = (bf16[48,4096]{1,0:T(8,128)(2,1)S(1)}, bf16[48,4096]{1,0:T(8,128)(2,1)S(1)}, u32[]{:S(2)}, u32[]{:S(2)}) collective-permute-start(bf16[48,4096]{1,0:T(8,128)(2,1)S(1)} %add_convert_fusion.6), channel_id=1, source_target_pairs={{0,1},{1,0},{2,3},{3,2},{4,5},{5,4},{6,7},{7,6},{8,9},{9,8},{10,11... | collective-permute-start | bytes 1179656 | tf_op jit(solution)/shard_map/ppermute | solution.py:30
  152.2 16.4 %all-to-all-start.2 = ((bf16[16,112,128]{2,1,0:T(8,128)(2,1)}), bf16[16,112,128]{2,1,0:T(8,128)(2,1)S(1)}, u32[]{:S(2)}, u32[]{:S(2)}) async-start(bf16[16,112,128]{2,1,0:T(8,128)(2,1)} %copy.38), calls=%async_computation.2 | async-start | bytes 917504 | tf_op jit(solution)/shard_map/all_to_all | solution.py:44
  168.6 24.4 %copy-start.3 = (bf16[384,4096]{1,0:T(8,128)(2,1)S(1)}, bf16[384,4096]{1,0:T(8,128)(2,1)}, u32[]{:S(2)}) copy-start(bf16[384,4096]{1,0:T(8,128)(2,1)} %copy-done.2) | copy-start | bytes 9437188
  171.5 24.0 %copy-start.1 = (bf16[256,4096]{1,0:T(8,128)(2,1)S(1)}, bf16[256,4096]{1,0:T(8,128)(2,1)}, u32[]{:S(2)}) copy-start(bf16[256,4096]{1,0:T(8,128)(2,1)} %proj_ref.1) | copy-start | bytes 6291460
  190.7 4.9 %collective-permute-start.28 = (bf16[16,256,128]{2,1,0:T(8,128)(2,1)S(1)}, bf16[16,256,128]{2,1,0:T(8,128)(2,1)S(1)}, u32[]{:S(2)}, u32[]{:S(2)}) collective-permute-start(bf16[16,256,128]{2,1,0:T(8,128)(2,1)S(1)} %all_to_all.20.mine_ref), channel_id=1, source_target_pairs={{0,1},{1,0},{2,3},{3,2},{4,5},{5,4},{6,7},{7,6},{8,9},{9,8},{10,11... | collective-permute-start | bytes 3145736 | tf_op jit(solution)/shard_map/ppermute | solution.py:30
Sparse Core Ops, SparseCore 0:
  11.9 48.5 all-gather.2

commit v2 on v1

--- a/solution.py
+++ b/solution.py
@@ -130,9 +130,10 @@
         (target[None, :, 0] == own_slots[:, None]) | (target[None, :, 1] == own_slots[:, None])
     ).astype(BF)
 
-    own_cots = jnp.dot(select, cotangent, preferred_element_type=F32).astype(BF)
+    cot_half = lax.dynamic_slice_in_dim(cotangent, core * half_width, half_width, 1)
+    own_cots = jnp.dot(select, cot_half, preferred_element_type=F32).astype(BF)
     mixer_out, own_cots = lax.optimization_barrier((mixer_out, own_cots))
-    all_cots = lax.all_gather(own_cots, "dp", axis=0)
+    all_cots = lax.all_gather(own_cots, ("dp", "group"), axis=0).reshape(8, 2, cap, half_width)
     term = jnp.dot(mixer_out, out_proj, preferred_element_type=F32).astype(BF)
     sent = lax.dynamic_slice_in_dim(term, (1 - core) * half_width, half_width, 1)
     kept = lax.dynamic_slice_in_dim(term, core * half_width, half_width, 1)
@@ -158,8 +159,9 @@
     inputs = jnp.concatenate(near + others + [far], axis=0)
     sign = 1 - 2 * core
     order = [z, z - sign, z - 2 * sign, z - 3 * sign, z + sign, z + 2 * sign, z + 3 * sign, z + 4]
+    cots = [lax.dynamic_index_in_dim(all_cots, (place + 8) % 8, 0, False) for place in order]
     cots = jnp.concatenate(
-        [lax.dynamic_index_in_dim(all_cots, (place + 8) % 8, 0, False) for place in order], axis=0
+        [jnp.concatenate((value[0], value[1]), axis=1) for value in cots], axis=0
     )
 
     own_router = lax.dynamic_index_in_dim(router.T, expert, 0, True)

time: 206 us -> 203 us (0.985)
  local copies, waits for them, and re-layouts: 9.35 us -> 6.45 us
    unnamed x31 -> x23, local copies, waits for them, and re-layouts: 5.41 us -> 1.21 us
    ppermute x12, starting transfers between devices: 13.8 us -> 16.7 us  [hop(): return lax.ppermute(value, ('dp', 'group'), pairs)]
    all_gather x1, waiting for transfers between devices: 2.83 us -> 0.49 us  [on_device(): lax.all_gather(own_cots, ('dp', 'group'), axis=0)]
    all_to_all x3, starting transfers between devices: 15.2 us -> 13 us  [exchange(): return lax.all_to_all(blocks, CHIPS, 0, 0)]
    ppermute x12, waiting for transfers between devices: 47.2 us -> 49.4 us  [hop(): return lax.ppermute(value, ('dp', 'group'), pairs)]
    squeeze x0 -> x1, local copies, waits for them, and re-layouts: none -> 2.16 us  [on_device(): value[0]]
where the time goes in v2:
time: 203 us
  waiting for transfers between devices  84.5 us (42%)
  starting transfers between devices  48.9 us (24%)
  matrix products  19.7 us (10%)
  blocking collectives  19.2 us (9%)
  between operations  14.8 us (7%)
  other arithmetic  6.62 us (3%)
  local copies, waits for them, and re-layouts  6.45 us (3%)
  Pallas kernels  2.54 us (1%)
    ppermute x12, waiting for transfers between devices, hop(): return lax.ppermute(value, ('dp', 'group'), pairs)  49.4 us
    all_to_all x3, waiting for transfers between devices, exchange(): return lax.all_to_all(blocks, CHIPS, 0, 0)  29.3 us
    all_to_all x1, blocking collectives, exchange(): return lax.all_to_all(blocks, CHIPS, 0, 0)  19.2 us
    ppermute x17, starting transfers between devices, swap_core(): return lax.ppermute(value, 'group', [(0, 1), (1, 0)])  19.1 us
    ppermute x12, starting transfers between devices, hop(): return lax.ppermute(value, ('dp', 'group'), pairs)  16.7 us
    all_to_all x3, starting transfers between devices, exchange(): return lax.all_to_all(blocks, CHIPS, 0, 0)  13 us
    ppermute x17, waiting for transfers between devices, swap_core(): return lax.ppermute(value, 'group', [(0, 1), (1, 0)])  5.22 us
    dot_general x4, matrix products, contract_cols(): lax.dot_general(left, right, (((1,), (1,)), ((), ())), preferred_element_...  4.62 us
  transfers between devices with their start and end apart: 33, of which 20 were waited for; matrix products, arithmetic and copies ran while one was open for 8% of the time, Pallas kernels for 0%

profile of v2, /device:TPU:1, one launch (start us, length us, event | category | flops | bytes accessed | tf_op | source)
XLA Modules:
  0.0 202.6 jit_solution(15496579025588651598)
XLA Ops:
  7.2 0.9 copy.33
  8.7 0.7 multiply_add_fusion.1
  9.4 2.0 convolution_convert_fusion.4
  11.4 2.1 %convolution_convert_fusion.2 = bf16[128,4096]{1,0:T(8,128)(2,1)S(1)} fusion(bf16[128,256]{1,0:T(8,128)(2,1)} %param.11, bf16[256,4096]{1,0:T(8,128)(2,1)} %proj_ref.1), kind=kOutput, calls=%fused_computation.5 | convolution fusion | flops 268959744 | bytes 3211264 | tf_op jit(solution)/shard_map/dot_general | solution.py:137
  13.6 3.3 %collective-permute-start = (bf16[128,2048]{1,0:T(8,128)(2,1)S(1)}, bf16[128,2048]{1,0:T(8,128)(2,1)S(1)}, u32[]{:S(2)}, u32[]{:S(2)}) collective-permute-start(bf16[128,2048]{1,0:T(8,128)(2,1)S(1)} %constant_dynamic-slice_fusion.4), channel_id=1, source_target_pairs={{0,1},{1,0},{2,3},{3,2},{4,5},{5,4},{6,7},{7,6},{8,9},{9,8},{10,11... | collective-permute-start | bytes 1572872 | tf_op jit(solution)/shard_map/ppermute | solution.py:30
  16.9 1.5 collective-permute-done
  18.4 1.0 bitcast_bitcast_fusion
  19.4 5.2 %all-to-all-start = ((bf16[16,128,128]{2,1,0:T(8,128)(2,1)}), bf16[16,128,128]{2,1,0:T(8,128)(2,1)S(1)}, u32[]{:S(2)}, u32[]{:S(2)}) async-start(bf16[16,128,128]{2,1,0:T(8,128)(2,1)} %bitcast_bitcast_fusion), calls=%async_computation | async-start | bytes 1048576 | tf_op jit(solution)/shard_map/all_to_all | solution.py:44
  24.6 10.7 %all-to-all-done = bf16[16,128,128]{2,1,0:T(8,128)(2,1)S(1)} async-done(((bf16[16,128,128]{2,1,0:T(8,128)(2,1)}), bf16[16,128,128]{2,1,0:T(8,128)(2,1)S(1)}, u32[]{:S(2)}, u32[]{:S(2)}) %all-to-all-start) | async-done | bytes 524320 | tf_op jit(solution)/shard_map/all_to_all | solution.py:44
  35.3 0.8 fusion.36
  36.1 0.9 broadcast_in_dim.13
  37.0 3.6 %all-to-all-start.1 = ((bf16[16,128,128]{2,1,0:T(8,128)(2,1)}), bf16[16,128,128]{2,1,0:T(8,128)(2,1)S(1)}, u32[]{:S(2)}, u32[]{:S(2)}) async-start(bf16[16,128,128]{2,1,0:T(8,128)(2,1)} %broadcast_in_dim.13), calls=%async_computation.1 | async-start | bytes 1048576 | tf_op jit(solution)/shard_map/all_to_all | solution.py:44
  40.7 0.9 reduce-precision_convert_fusion.1
  41.7 8.9 %all-to-all-done.1 = bf16[16,128,128]{2,1,0:T(8,128)(2,1)S(1)} async-done(((bf16[16,128,128]{2,1,0:T(8,128)(2,1)}), bf16[16,128,128]{2,1,0:T(8,128)(2,1)S(1)}, u32[]{:S(2)}, u32[]{:S(2)}) %all-to-all-start.1) | async-done | bytes 524320 | tf_op jit(solution)/shard_map/all_to_all | solution.py:44
  50.9 2.6 %collective-permute-start.1 = (bf16[16,128,128]{1,2,0:T(8,128)(2,1)S(1)}, bf16[16,128,128]{1,2,0:T(8,128)(2,1)S(1)}, u32[]{:S(2)}, u32[]{:S(2)}) collective-permute-start(bf16[16,128,128]{1,2,0:T(8,128)(2,1)S(1)} %copy.36), channel_id=1, source_target_pairs={{0,1},{1,0},{2,3},{3,2},{4,5},{5,4},{6,7},{7,6},{8,9},{9,8},{10,11... | collective-permute-start | bytes 1572872 | tf_op jit(solution)/shard_map/ppermute | solution.py:30
  53.5 1.5 collective-permute-done.1
  55.0 0.6 fusion.1
  55.6 0.8 convolution_convert_fusion.3
  56.4 0.5 all-gather.3.cloned.1.call-done
  56.9 5.2 %collective-permute-start.2 = (bf16[48,4096]{1,0:T(8,128)(2,1)S(1)}, bf16[48,4096]{1,0:T(8,128)(2,1)S(1)}, u32[]{:S(2)}, u32[]{:S(2)}) collective-permute-start(bf16[48,4096]{1,0:T(8,128)(2,1)S(1)} %convolution_convert_fusion.3), channel_id=1, source_target_pairs={{0,32},{1,225},{32,64},{33,1},{64,96},{65,33},{96,128},{97,65},{12... | collective-permute-start | bytes 1179656 | tf_op jit(solution)/shard_map/ppermute | solution.py:40
  62.1 2.2 %dynamic-slice_bitcast_fusion.1 = (bf16[48,2048]{1,0:T(8,128)(2,1)S(1)}, bf16[48,2048]{1,0:T(8,128)(2,1)S(1)}, bf16[48,2048]{1,0:T(8,128)(2,1)S(1)}, bf16[48,204...) fusion(bf16[8,2,48,2048]{3,2,1,0:T(8,128)(2,1)} %bitcast.98, ...), kind=kLoop, calls=%fused_computation.78 | loop fusion | bytes 6291492 | tf_op jit(solution)/shard_map/squeeze | solution.py:164
  64.6 2.3 %collective-permute-done.2 = bf16[48,4096]{1,0:T(8,128)(2,1)S(1)} collective-permute-done((bf16[48,4096]{1,0:T(8,128)(2,1)S(1)}, bf16[48,4096]{1,0:T(8,128)(2,1)S(1)}, u32[]{:S(2)}, u32[]{:S(2)}) %collective-permute-start.2) | collective-permute-done | bytes 393248 | tf_op jit(solution)/shard_map/ppermute | solution.py:40
  66.8 3.1 %collective-permute-start.3 = (bf16[48,4096]{1,0:T(8,128)(2,1)S(1)}, bf16[48,4096]{1,0:T(8,128)(2,1)S(1)}, u32[]{:S(2)}, u32[]{:S(2)}) collective-permute-start(bf16[48,4096]{1,0:T(8,128)(2,1)S(1)} %collective-permute-done.2), channel_id=1, source_target_pairs={{0,32},{1,225},{32,64},{33,1},{64,96},{65,33},{96,128},{97,65},{12... | collective-permute-start | bytes 1179656 | tf_op jit(solution)/shard_map/ppermute | solution.py:40
  70.0 4.7 %collective-permute-done.3 = bf16[48,4096]{1,0:T(8,128)(2,1)S(1)} collective-permute-done((bf16[48,4096]{1,0:T(8,128)(2,1)S(1)}, bf16[48,4096]{1,0:T(8,128)(2,1)S(1)}, u32[]{:S(2)}, u32[]{:S(2)}) %collective-permute-start.3) | collective-permute-done | bytes 393248 | tf_op jit(solution)/shard_map/ppermute | solution.py:40
  74.7 3.1 %collective-permute-start.4 = (bf16[48,4096]{1,0:T(8,128)(2,1)S(1)}, bf16[48,4096]{1,0:T(8,128)(2,1)S(1)}, u32[]{:S(2)}, u32[]{:S(2)}) collective-permute-start(bf16[48,4096]{1,0:T(8,128)(2,1)S(1)} %collective-permute-done.3), channel_id=1, source_target_pairs={{0,32},{1,225},{32,64},{33,1},{64,96},{65,33},{96,128},{97,65},{12... | collective-permute-start | bytes 1179656 | tf_op jit(solution)/shard_map/ppermute | solution.py:40
  77.8 4.7 %collective-permute-done.4 = bf16[48,4096]{1,0:T(8,128)(2,1)S(1)} collective-permute-done((bf16[48,4096]{1,0:T(8,128)(2,1)S(1)}, bf16[48,4096]{1,0:T(8,128)(2,1)S(1)}, u32[]{:S(2)}, u32[]{:S(2)}) %collective-permute-start.4) | collective-permute-done | bytes 393248 | tf_op jit(solution)/shard_map/ppermute | solution.py:40
  82.5 3.2 %collective-permute-start.8 = (bf16[48,2048]{1,0:T(8,128)(2,1)S(1)}, bf16[48,2048]{1,0:T(8,128)(2,1)S(1)}, u32[]{:S(2)}, u32[]{:S(2)}) collective-permute-start(bf16[48,2048]{1,0:T(8,128)(2,1)S(1)} %constant_dynamic-slice_fusion.3), channel_id=1, source_target_pairs={{0,32},{1,225},{32,64},{33,1},{64,96},{65,33},{96,128},{97,65},{12... | collective-permute-start | bytes 589832 | tf_op jit(solution)/shard_map/ppermute | solution.py:40
  85.7 1.0 collective-permute-start.7
  86.8 1.5 collective-permute-done.8
  88.3 5.1 %collective-permute-start.9 = (bf16[48,2048]{1,0:T(8,128)(2,1)S(1)}, bf16[48,2048]{1,0:T(8,128)(2,1)S(1)}, u32[]{:S(2)}, u32[]{:S(2)}) collective-permute-start(bf16[48,2048]{1,0:T(8,128)(2,1)S(1)} %collective-permute-done.8), channel_id=1, source_target_pairs={{0,1},{1,0},{2,3},{3,2},{4,5},{5,4},{6,7},{7,6},{8,9},{9,8},{10,11... | collective-permute-start | bytes 589832 | tf_op jit(solution)/shard_map/ppermute | solution.py:30
  93.5 1.0 collective-permute-done.9
  94.7 1.2 fusion.12
  95.9 1.2 fusion.8
  97.1 0.9 convolution_reduce_fusion
  98.1 1.3 multiply_reduce_fusion.1
  99.4 1.0 convolution_convert_fusion
  100.6 1.1 fusion.10
  101.7 1.2 add_convert_fusion
  103.1 0.5 collective-permute-start.19
  103.8 0.4 collective-permute-start.12
  104.3 0.4 collective-permute-start.16
  104.7 0.3 collective-permute-start.21
  105.2 5.7 %collective-permute-done.20 = bf16[48,2048]{1,0:T(8,128)(2,1)S(1)} collective-permute-done((bf16[48,2048]{1,0:T(8,128)(2,1)S(1)}, bf16[48,2048]{1,0:T(8,128)(2,1)S(1)}, u32[]{:S(2)}, u32[]{:S(2)}) %collective-permute-start.20) | collective-permute-done | bytes 196640 | tf_op jit(solution)/shard_map/ppermute | solution.py:40
  111.5 5.6 %collective-permute-done.11 = bf16[48,2048]{1,0:T(8,128)(2,1)S(1)} collective-permute-done((bf16[48,2048]{1,0:T(8,128)(2,1)S(1)}, bf16[48,2048]{1,0:T(8,128)(2,1)S(1)}, u32[]{:S(2)}, u32[]{:S(2)}) %collective-permute-start.11) | collective-permute-done | bytes 196640 | tf_op jit(solution)/shard_map/ppermute | solution.py:40
  117.1 0.3 collective-permute-start.25
  117.7 1.3 collective-permute-start.13
  119.0 6.3 %collective-permute-done.22 = bf16[48,4096]{1,0:T(8,128)(2,1)S(1)} collective-permute-done((bf16[48,4096]{1,0:T(8,128)(2,1)S(1)}, bf16[48,4096]{1,0:T(8,128)(2,1)S(1)}, u32[]{:S(2)}, u32[]{:S(2)}) %collective-permute-start.22) | collective-permute-done | bytes 393248 | tf_op jit(solution)/shard_map/ppermute | solution.py:40
  125.6 4.0 %collective-permute-done.13 = bf16[48,4096]{1,0:T(8,128)(2,1)S(1)} collective-permute-done((bf16[48,4096]{1,0:T(8,128)(2,1)S(1)}, bf16[48,4096]{1,0:T(8,128)(2,1)S(1)}, u32[]{:S(2)}, u32[]{:S(2)}) %collective-permute-start.13) | collective-permute-done | bytes 393248 | tf_op jit(solution)/shard_map/ppermute | solution.py:40
  129.8 4.0 %collective-permute-done.24 = bf16[48,4096]{1,0:T(8,128)(2,1)S(1)} collective-permute-done((bf16[48,4096]{1,0:T(8,128)(2,1)S(1)}, bf16[48,4096]{1,0:T(8,128)(2,1)S(1)}, u32[]{:S(2)}, u32[]{:S(2)}) %collective-permute-start.24) | collective-permute-done | bytes 393248 | tf_op jit(solution)/shard_map/ppermute | solution.py:40
  134.0 4.0 %collective-permute-done.15 = bf16[48,4096]{1,0:T(8,128)(2,1)S(1)} collective-permute-done((bf16[48,4096]{1,0:T(8,128)(2,1)S(1)}, bf16[48,4096]{1,0:T(8,128)(2,1)S(1)}, u32[]{:S(2)}, u32[]{:S(2)}) %collective-permute-start.15) | collective-permute-done | bytes 393248 | tf_op jit(solution)/shard_map/ppermute | solution.py:40
  138.2 4.0 %collective-permute-done.26 = bf16[48,4096]{1,0:T(8,128)(2,1)S(1)} collective-permute-done((bf16[48,4096]{1,0:T(8,128)(2,1)S(1)}, bf16[48,4096]{1,0:T(8,128)(2,1)S(1)}, u32[]{:S(2)}, u32[]{:S(2)}) %collective-permute-start.26) | collective-permute-done | bytes 393248 | tf_op jit(solution)/shard_map/ppermute | solution.py:40
  142.3 1.2 collective-permute-start.27
  143.5 2.9 %collective-permute-done.17 = bf16[48,4096]{1,0:T(8,128)(2,1)S(1)} collective-permute-done((bf16[48,4096]{1,0:T(8,128)(2,1)S(1)}, bf16[48,4096]{1,0:T(8,128)(2,1)S(1)}, u32[]{:S(2)}, u32[]{:S(2)}) %collective-permute-start.17) | collective-permute-done | bytes 393248 | tf_op jit(solution)/shard_map/ppermute | solution.py:40
  146.5 1.2 collective-permute-start.18
  148.0 1.1 collective-permute-done.18
  149.4 0.9 copy.38
  150.3 4.3 %all-to-all-start.2 = ((bf16[16,112,128]{2,1,0:T(8,128)(2,1)}), bf16[16,112,128]{2,1,0:T(8,128)(2,1)S(1)}, u32[]{:S(2)}, u32[]{:S(2)}) async-start(bf16[16,112,128]{2,1,0:T(8,128)(2,1)} %copy.38), calls=%async_computation.2 | async-start | bytes 917504 | tf_op jit(solution)/shard_map/all_to_all | solution.py:44
  154.8 9.7 %all-to-all-done.2 = bf16[16,112,128]{2,1,0:T(8,128)(2,1)S(1)} async-done(((bf16[16,112,128]{2,1,0:T(8,128)(2,1)}), bf16[16,112,128]{2,1,0:T(8,128)(2,1)S(1)}, u32[]{:S(2)}, u32[]{:S(2)}) %all-to-all-start.2) | async-done | bytes 458784 | tf_op jit(solution)/shard_map/all_to_all | solution.py:44
  164.9 1.1 fusion.17
  165.9 1.1 fusion.18
  167.2 19.2 %all_to_all.20.mine_ref = bf16[16,256,128]{2,1,0:T(8,128)(2,1)S(1)} all-to-all(bf16[16,256,128]{2,1,0:T(8,128)(2,1)S(1)} %broadcast_in_dim.16), channel_id=1, replica_groups=mesh['dp'=8,'y'=4,'xh'=2,'half'=2,'group'=2] {'y','xh','half'}, dimensions={0} | all-to-all | bytes 2097152 | tf_op jit(solution)/shard_map/all_to_all | solution.py:44
  186.4 2.4 %collective-permute-start.28 = (bf16[16,256,128]{2,1,0:T(8,128)(2,1)S(1)}, bf16[16,256,128]{2,1,0:T(8,128)(2,1)S(1)}, u32[]{:S(2)}, u32[]{:S(2)}) collective-permute-start(bf16[16,256,128]{2,1,0:T(8,128)(2,1)S(1)} %all_to_all.20.mine_ref), channel_id=1, source_target_pairs={{0,1},{1,0},{2,3},{3,2},{4,5},{5,4},{6,7},{7,6},{8,9},{9,8},{10,11... | collective-permute-start | bytes 3145736 | tf_op jit(solution)/shard_map/ppermute | solution.py:30
  188.8 4.5 %fusion = bf16[1,224,4096]{2,1,0:T(8,128)(2,1)} fusion(bf16[384,224]{0,1:T(8,128)(2,1)S(1)} %get-tuple-element.16, bf16[384,4096]{1,0:T(8,128)(2,1)} %copy-done.3, f32[384]{0:T(512)S(1)} %add_divide_fusion.1), kind=kOutput, calls=%fused_computation.4 | convolution fusion | flops 710279168 | bytes 5154304 | tf_op jit(solution)/shard_map/dot_general | solution.py:14
  193.2 2.5 %shard_map.121 = (bf16[128,4096]{1,0:T(8,128)(2,1)}, bf16[128,256]{1,0:T(8,128)(2,1)}) custom-call(s32[1]{0:T(128)} %bitcast.core_ref, bf16[16,256,128]{2,1,0:T(8,128)(2,1)S(1)} %all_to_all.20.mine_ref, bf16[16,256,128]{2,1,0:T(8,128)(2,1)S(1)} %collective-permute-done.28.other_ref, bf16[256,4096]{1,0:T(8,128)(2,1)S(1)} %copy-done.2), custom_call_target="tpu_custom_call" | custom-call | tf_op jit(solution)/shard_map/pallas_call | solution.py:91
  (108 shorter events, 5.9 us)
Async XLA Ops:
  7.2 90.9 %copy-start = (bf16[1,224,4096]{2,1,0:T(8,128)(2,1)S(1)}, bf16[1,224,4096]{2,1,0:T(8,128)(2,1)}, u32[]{:S(2)}) copy-start(bf16[1,224,4096]{2,1,0:T(8,128)(2,1)} %param.18) | copy-start | bytes 5505028
  7.2 49.7 %all-gather.3.cloned.1.call-start = ((), (), s32[]{:S(2)}) async-start(), calls=%async_computation.4 | async-start | bytes 3342336 | tf_op jit(solution)/shard_map/all_gather | solution.py:136
  13.6 4.9 %collective-permute-start = (bf16[128,2048]{1,0:T(8,128)(2,1)S(1)}, bf16[128,2048]{1,0:T(8,128)(2,1)S(1)}, u32[]{:S(2)}, u32[]{:S(2)}) collective-permute-start(bf16[128,2048]{1,0:T(8,128)(2,1)S(1)} %constant_dynamic-slice_fusion.4), channel_id=1, source_target_pairs={{0,1},{1,0},{2,3},{3,2},{4,5},{5,4},{6,7},{7,6},{8,9},{9,8},{10,11... | collective-permute-start | bytes 1572872 | tf_op jit(solution)/shard_map/ppermute | solution.py:30
  19.4 36.2 %copy-start.6 = (f32[4096]{0:T(1024)S(1)}, f32[4096]{0:T(1024)}, u32[]{:S(2)}) copy-start(f32[4096]{0:T(1024)} %param.13) | copy-start | bytes 49156
  19.4 15.9 %all-to-all-start = ((bf16[16,128,128]{2,1,0:T(8,128)(2,1)}), bf16[16,128,128]{2,1,0:T(8,128)(2,1)S(1)}, u32[]{:S(2)}, u32[]{:S(2)}) async-start(bf16[16,128,128]{2,1,0:T(8,128)(2,1)} %bitcast_bitcast_fusion), calls=%async_computation | async-start | bytes 1048576 | tf_op jit(solution)/shard_map/all_to_all | solution.py:44
  37.0 13.6 %all-to-all-start.1 = ((bf16[16,128,128]{2,1,0:T(8,128)(2,1)}), bf16[16,128,128]{2,1,0:T(8,128)(2,1)S(1)}, u32[]{:S(2)}, u32[]{:S(2)}) async-start(bf16[16,128,128]{2,1,0:T(8,128)(2,1)} %broadcast_in_dim.13), calls=%async_computation.1 | async-start | bytes 1048576 | tf_op jit(solution)/shard_map/all_to_all | solution.py:44
  50.9 4.1 %collective-permute-start.1 = (bf16[16,128,128]{1,2,0:T(8,128)(2,1)S(1)}, bf16[16,128,128]{1,2,0:T(8,128)(2,1)S(1)}, u32[]{:S(2)}, u32[]{:S(2)}) collective-permute-start(bf16[16,128,128]{1,2,0:T(8,128)(2,1)S(1)} %copy.36), channel_id=1, source_target_pairs={{0,1},{1,0},{2,3},{3,2},{4,5},{5,4},{6,7},{7,6},{8,9},{9,8},{10,11... | collective-permute-start | bytes 1572872 | tf_op jit(solution)/shard_map/ppermute | solution.py:30
  56.9 9.9 %collective-permute-start.2 = (bf16[48,4096]{1,0:T(8,128)(2,1)S(1)}, bf16[48,4096]{1,0:T(8,128)(2,1)S(1)}, u32[]{:S(2)}, u32[]{:S(2)}) collective-permute-start(bf16[48,4096]{1,0:T(8,128)(2,1)S(1)} %convolution_convert_fusion.3), channel_id=1, source_target_pairs={{0,32},{1,225},{32,64},{33,1},{64,96},{65,33},{96,128},{97,65},{12... | collective-permute-start | bytes 1179656 | tf_op jit(solution)/shard_map/ppermute | solution.py:40
  64.6 33.5 %copy-start.3 = (bf16[384,4096]{1,0:T(8,128)(2,1)}, bf16[384,4096]{1,0:T(8,128)(2,1)S(1)}, u32[]{:S(2)}) copy-start(bf16[384,4096]{1,0:T(8,128)(2,1)S(1)} %maximum_dynamic-update-slice_fusion) | copy-start | bytes 9437188
  64.6 30.1 %copy-start.5 = (bf16[1,4096,224]{1,2,0:T(8,128)(2,1)S(1)}, bf16[1,4096,224]{1,2,0:T(8,128)(2,1)}, u32[]{:S(2)}) copy-start(bf16[1,4096,224]{1,2,0:T(8,128)(2,1)} %param.16) | copy-start | bytes 5505028
  66.8 7.8 %collective-permute-start.3 = (bf16[48,4096]{1,0:T(8,128)(2,1)S(1)}, bf16[48,4096]{1,0:T(8,128)(2,1)S(1)}, u32[]{:S(2)}, u32[]{:S(2)}) collective-permute-start(bf16[48,4096]{1,0:T(8,128)(2,1)S(1)} %collective-permute-done.2), channel_id=1, source_target_pairs={{0,32},{1,225},{32,64},{33,1},{64,96},{65,33},{96,128},{97,65},{12... | collective-permute-start | bytes 1179656 | tf_op jit(solution)/shard_map/ppermute | solution.py:40
  70.0 16.8 %collective-permute-start.5 = (bf16[48,4096]{1,0:T(8,128)(2,1)S(1)}, bf16[48,4096]{1,0:T(8,128)(2,1)S(1)}, u32[]{:S(2)}, u32[]{:S(2)}) collective-permute-start(bf16[48,4096]{1,0:T(8,128)(2,1)S(1)} %collective-permute-done.2), channel_id=1, source_target_pairs={{0,1},{1,0},{2,3},{3,2},{4,5},{5,4},{6,7},{7,6},{8,9},{9,8},{10,11... | collective-permute-start | bytes 1179656 | tf_op jit(solution)/shard_map/ppermute | solution.py:30
  74.7 7.8 %collective-permute-start.4 = (bf16[48,4096]{1,0:T(8,128)(2,1)S(1)}, bf16[48,4096]{1,0:T(8,128)(2,1)S(1)}, u32[]{:S(2)}, u32[]{:S(2)}) collective-permute-start(bf16[48,4096]{1,0:T(8,128)(2,1)S(1)} %collective-permute-done.3), channel_id=1, source_target_pairs={{0,32},{1,225},{32,64},{33,1},{64,96},{65,33},{96,128},{97,65},{12... | collective-permute-start | bytes 1179656 | tf_op jit(solution)/shard_map/ppermute | solution.py:40
  77.8 9.0 %collective-permute-start.6 = (bf16[48,4096]{1,0:T(8,128)(2,1)S(1)}, bf16[48,4096]{1,0:T(8,128)(2,1)S(1)}, u32[]{:S(2)}, u32[]{:S(2)}) collective-permute-start(bf16[48,4096]{1,0:T(8,128)(2,1)S(1)} %collective-permute-done.3), channel_id=1, source_target_pairs={{0,1},{1,0},{2,3},{3,2},{4,5},{5,4},{6,7},{7,6},{8,9},{9,8},{10,11... | collective-permute-start | bytes 1179656 | tf_op jit(solution)/shard_map/ppermute | solution.py:30
  82.5 5.8 %collective-permute-start.8 = (bf16[48,2048]{1,0:T(8,128)(2,1)S(1)}, bf16[48,2048]{1,0:T(8,128)(2,1)S(1)}, u32[]{:S(2)}, u32[]{:S(2)}) collective-permute-start(bf16[48,2048]{1,0:T(8,128)(2,1)S(1)} %constant_dynamic-slice_fusion.3), channel_id=1, source_target_pairs={{0,32},{1,225},{32,64},{33,1},{64,96},{65,33},{96,128},{97,65},{12... | collective-permute-start | bytes 589832 | tf_op jit(solution)/shard_map/ppermute | solution.py:40
  85.7 7.8 %collective-permute-start.7 = (bf16[48,4096]{1,0:T(8,128)(2,1)S(1)}, bf16[48,4096]{1,0:T(8,128)(2,1)S(1)}, u32[]{:S(2)}, u32[]{:S(2)}) collective-permute-start(bf16[48,4096]{1,0:T(8,128)(2,1)S(1)} %collective-permute-done.4), channel_id=1, source_target_pairs={{0,1},{1,0},{2,3},{3,2},{4,5},{5,4},{6,7},{7,6},{8,9},{9,8},{10,11... | collective-permute-start | bytes 1179656 | tf_op jit(solution)/shard_map/ppermute | solution.py:30
  88.3 6.2 %collective-permute-start.9 = (bf16[48,2048]{1,0:T(8,128)(2,1)S(1)}, bf16[48,2048]{1,0:T(8,128)(2,1)S(1)}, u32[]{:S(2)}, u32[]{:S(2)}) collective-permute-start(bf16[48,2048]{1,0:T(8,128)(2,1)S(1)} %collective-permute-done.8), channel_id=1, source_target_pairs={{0,1},{1,0},{2,3},{3,2},{4,5},{5,4},{6,7},{7,6},{8,9},{9,8},{10,11... | collective-permute-start | bytes 589832 | tf_op jit(solution)/shard_map/ppermute | solution.py:30
  93.5 2.4 %copy-start.4 = (bf16[1,4096,224]{1,2,0:T(8,128)(2,1)S(1)}, bf16[1,4096,224]{1,2,0:T(8,128)(2,1)}, u32[]{:S(2)}) copy-start(bf16[1,4096,224]{1,2,0:T(8,128)(2,1)} %param.17) | copy-start | bytes 5505028
  103.1 1.6 collective-permute-start.19
  103.6 1.5 collective-permute-start.10
  103.8 13.6 %collective-permute-start.12 = (bf16[48,4096]{1,0:T(8,128)(2,1)S(1)}, bf16[48,4096]{1,0:T(8,128)(2,1)S(1)}, u32[]{:S(2)}, u32[]{:S(2)}) collective-permute-start(bf16[48,4096]{1,0:T(8,128)(2,1)S(1)} %get-tuple-element.22), channel_id=1, source_target_pairs={{0,1},{1,0},{2,3},{3,2},{4,5},{5,4},{6,7},{7,6},{8,9},{9,8},{10,11... | collective-permute-start | bytes 1179656 | tf_op jit(solution)/shard_map/ppermute | solution.py:30
  104.2 21.4 %collective-permute-start.14 = (bf16[48,4096]{1,0:T(8,128)(2,1)S(1)}, bf16[48,4096]{1,0:T(8,128)(2,1)S(1)}, u32[]{:S(2)}, u32[]{:S(2)}) collective-permute-start(bf16[48,4096]{1,0:T(8,128)(2,1)S(1)} %get-tuple-element.21), channel_id=1, source_target_pairs={{0,1},{1,0},{2,3},{3,2},{4,5},{5,4},{6,7},{7,6},{8,9},{9,8},{10,11... | collective-permute-start | bytes 1179656 | tf_op jit(solution)/shard_map/ppermute | solution.py:30
  104.3 29.7 %collective-permute-start.16 = (bf16[48,4096]{1,0:T(8,128)(2,1)S(1)}, bf16[48,4096]{1,0:T(8,128)(2,1)S(1)}, u32[]{:S(2)}, u32[]{:S(2)}) collective-permute-start(bf16[48,4096]{1,0:T(8,128)(2,1)S(1)} %get-tuple-element.20), channel_id=1, source_target_pairs={{0,1},{1,0},{2,3},{3,2},{4,5},{5,4},{6,7},{7,6},{8,9},{9,8},{10,11... | collective-permute-start | bytes 1179656 | tf_op jit(solution)/shard_map/ppermute | solution.py:30
  104.7 6.4 %collective-permute-start.21 = (bf16[48,4096]{1,0:T(8,128)(2,1)S(1)}, bf16[48,4096]{1,0:T(8,128)(2,1)S(1)}, u32[]{:S(2)}, u32[]{:S(2)}) collective-permute-start(bf16[48,4096]{1,0:T(8,128)(2,1)S(1)} %get-tuple-element.26), channel_id=1, source_target_pairs={{0,1},{1,0},{2,3},{3,2},{4,5},{5,4},{6,7},{7,6},{8,9},{9,8},{10,11... | collective-permute-start | bytes 1179656 | tf_op jit(solution)/shard_map/ppermute | solution.py:30
  105.1 5.8 %collective-permute-start.20 = (bf16[48,2048]{1,0:T(8,128)(2,1)S(1)}, bf16[48,2048]{1,0:T(8,128)(2,1)S(1)}, u32[]{:S(2)}, u32[]{:S(2)}) collective-permute-start(bf16[48,2048]{1,0:T(8,128)(2,1)S(1)} %add_convert_fusion.10), channel_id=1, source_target_pairs={{0,224},{1,33},{32,0},{33,65},{64,32},{65,97},{96,64},{97,129},{12... | collective-permute-start | bytes 589832 | tf_op jit(solution)/shard_map/ppermute | solution.py:40
  110.9 6.8 %collective-permute-start.23 = (bf16[48,4096]{1,0:T(8,128)(2,1)S(1)}, bf16[48,4096]{1,0:T(8,128)(2,1)S(1)}, u32[]{:S(2)}, u32[]{:S(2)}) collective-permute-start(bf16[48,4096]{1,0:T(8,128)(2,1)S(1)} %get-tuple-element.25), channel_id=1, source_target_pairs={{0,1},{1,0},{2,3},{3,2},{4,5},{5,4},{6,7},{7,6},{8,9},{9,8},{10,11... | collective-permute-start | bytes 1179656 | tf_op jit(solution)/shard_map/ppermute | solution.py:30
  111.0 6.0 %collective-permute-start.11 = (bf16[48,2048]{1,0:T(8,128)(2,1)S(1)}, bf16[48,2048]{1,0:T(8,128)(2,1)S(1)}, u32[]{:S(2)}, u32[]{:S(2)}) collective-permute-start(bf16[48,2048]{1,0:T(8,128)(2,1)S(1)} %add_convert_fusion.11), channel_id=1, source_target_pairs={{0,224},{1,33},{32,0},{33,65},{64,32},{65,97},{96,64},{97,129},{12... | collective-permute-start | bytes 589832 | tf_op jit(solution)/shard_map/ppermute | solution.py:40
  117.1 12.7 %collective-permute-start.25 = (bf16[48,4096]{1,0:T(8,128)(2,1)S(1)}, bf16[48,4096]{1,0:T(8,128)(2,1)S(1)}, u32[]{:S(2)}, u32[]{:S(2)}) collective-permute-start(bf16[48,4096]{1,0:T(8,128)(2,1)S(1)} %get-tuple-element.24), channel_id=1, source_target_pairs={{0,1},{1,0},{2,3},{3,2},{4,5},{5,4},{6,7},{7,6},{8,9},{9,8},{10,11... | collective-permute-start | bytes 1179656 | tf_op jit(solution)/shard_map/ppermute | solution.py:30
  117.4 7.9 %collective-permute-start.22 = (bf16[48,4096]{1,0:T(8,128)(2,1)S(1)}, bf16[48,4096]{1,0:T(8,128)(2,1)S(1)}, u32[]{:S(2)}, u32[]{:S(2)}) collective-permute-start(bf16[48,4096]{1,0:T(8,128)(2,1)S(1)} %add_convert_fusion.5), channel_id=1, source_target_pairs={{0,224},{1,33},{32,0},{33,65},{64,32},{65,97},{96,64},{97,129},{12... | collective-permute-start | bytes 1179656 | tf_op jit(solution)/shard_map/ppermute | solution.py:40
  117.7 11.9 %collective-permute-start.13 = (bf16[48,4096]{1,0:T(8,128)(2,1)S(1)}, bf16[48,4096]{1,0:T(8,128)(2,1)S(1)}, u32[]{:S(2)}, u32[]{:S(2)}) collective-permute-start(bf16[48,4096]{1,0:T(8,128)(2,1)S(1)} %add_convert_fusion.9), channel_id=1, source_target_pairs={{0,224},{1,33},{32,0},{33,65},{64,32},{65,97},{96,64},{97,129},{12... | collective-permute-start | bytes 1179656 | tf_op jit(solution)/shard_map/ppermute | solution.py:40
  125.5 8.3 %collective-permute-start.24 = (bf16[48,4096]{1,0:T(8,128)(2,1)S(1)}, bf16[48,4096]{1,0:T(8,128)(2,1)S(1)}, u32[]{:S(2)}, u32[]{:S(2)}) collective-permute-start(bf16[48,4096]{1,0:T(8,128)(2,1)S(1)} %add_convert_fusion.4), channel_id=1, source_target_pairs={{0,224},{1,33},{32,0},{33,65},{64,32},{65,97},{96,64},{97,129},{12... | collective-permute-start | bytes 1179656 | tf_op jit(solution)/shard_map/ppermute | solution.py:40
  129.7 8.3 %collective-permute-start.15 = (bf16[48,4096]{1,0:T(8,128)(2,1)S(1)}, bf16[48,4096]{1,0:T(8,128)(2,1)S(1)}, u32[]{:S(2)}, u32[]{:S(2)}) collective-permute-start(bf16[48,4096]{1,0:T(8,128)(2,1)S(1)} %add_convert_fusion.8), channel_id=1, source_target_pairs={{0,224},{1,33},{32,0},{33,65},{64,32},{65,97},{96,64},{97,129},{12... | collective-permute-start | bytes 1179656 | tf_op jit(solution)/shard_map/ppermute | solution.py:40
  133.9 8.3 %collective-permute-start.26 = (bf16[48,4096]{1,0:T(8,128)(2,1)S(1)}, bf16[48,4096]{1,0:T(8,128)(2,1)S(1)}, u32[]{:S(2)}, u32[]{:S(2)}) collective-permute-start(bf16[48,4096]{1,0:T(8,128)(2,1)S(1)} %add_convert_fusion.3), channel_id=1, source_target_pairs={{0,224},{1,33},{32,0},{33,65},{64,32},{65,97},{96,64},{97,129},{12... | collective-permute-start | bytes 1179656 | tf_op jit(solution)/shard_map/ppermute | solution.py:40
  138.1 8.3 %collective-permute-start.17 = (bf16[48,4096]{1,0:T(8,128)(2,1)S(1)}, bf16[48,4096]{1,0:T(8,128)(2,1)S(1)}, u32[]{:S(2)}, u32[]{:S(2)}) collective-permute-start(bf16[48,4096]{1,0:T(8,128)(2,1)S(1)} %add_convert_fusion.7), channel_id=1, source_target_pairs={{0,224},{1,33},{32,0},{33,65},{64,32},{65,97},{96,64},{97,129},{12... | collective-permute-start | bytes 1179656 | tf_op jit(solution)/shard_map/ppermute | solution.py:40
  142.3 5.4 %collective-permute-start.27 = (bf16[48,4096]{1,0:T(8,128)(2,1)S(1)}, bf16[48,4096]{1,0:T(8,128)(2,1)S(1)}, u32[]{:S(2)}, u32[]{:S(2)}) collective-permute-start(bf16[48,4096]{1,0:T(8,128)(2,1)S(1)} %add_convert_fusion.2), channel_id=1, source_target_pairs={{0,1},{1,0},{2,3},{3,2},{4,5},{5,4},{6,7},{7,6},{8,9},{9,8},{10,11... | collective-permute-start | bytes 1179656 | tf_op jit(solution)/shard_map/ppermute | solution.py:30
  146.5 2.5 %collective-permute-start.18 = (bf16[48,4096]{1,0:T(8,128)(2,1)S(1)}, bf16[48,4096]{1,0:T(8,128)(2,1)S(1)}, u32[]{:S(2)}, u32[]{:S(2)}) collective-permute-start(bf16[48,4096]{1,0:T(8,128)(2,1)S(1)} %add_convert_fusion.6), channel_id=1, source_target_pairs={{0,1},{1,0},{2,3},{3,2},{4,5},{5,4},{6,7},{7,6},{8,9},{9,8},{10,11... | collective-permute-start | bytes 1179656 | tf_op jit(solution)/shard_map/ppermute | solution.py:30
  150.3 14.2 %all-to-all-start.2 = ((bf16[16,112,128]{2,1,0:T(8,128)(2,1)}), bf16[16,112,128]{2,1,0:T(8,128)(2,1)S(1)}, u32[]{:S(2)}, u32[]{:S(2)}) async-start(bf16[16,112,128]{2,1,0:T(8,128)(2,1)} %copy.38), calls=%async_computation.2 | async-start | bytes 917504 | tf_op jit(solution)/shard_map/all_to_all | solution.py:44
  167.2 26.0 %copy-start.2 = (bf16[256,4096]{1,0:T(8,128)(2,1)S(1)}, bf16[256,4096]{1,0:T(8,128)(2,1)}, u32[]{:S(2)}) copy-start(bf16[256,4096]{1,0:T(8,128)(2,1)} %proj_ref.1) | copy-start | bytes 6291460
  186.4 6.8 %collective-permute-start.28 = (bf16[16,256,128]{2,1,0:T(8,128)(2,1)S(1)}, bf16[16,256,128]{2,1,0:T(8,128)(2,1)S(1)}, u32[]{:S(2)}, u32[]{:S(2)}) collective-permute-start(bf16[16,256,128]{2,1,0:T(8,128)(2,1)S(1)} %all_to_all.20.mine_ref), channel_id=1, source_target_pairs={{0,1},{1,0},{2,3},{3,2},{4,5},{5,4},{6,7},{7,6},{8,9},{9,8},{10,11... | collective-permute-start | bytes 3145736 | tf_op jit(solution)/shard_map/ppermute | solution.py:30
  188.7 7.0 %copy-start.1 = (bf16[1,224,4096]{2,1,0:T(8,128)(2,1)S(1)}, bf16[1,224,4096]{2,1,0:T(8,128)(2,1)}, u32[]{:S(2)}) copy-start(bf16[1,224,4096]{2,1,0:T(8,128)(2,1)} %param.18) | copy-start | bytes 5505028
Sparse Core Ops, SparseCore 0:
  11.6 45.2 all-gather.2

commit v3 on v2

--- a/solution.py
+++ b/solution.py
@@ -201,6 +201,7 @@
 
     half_out = collect(out_part)
     half_in = collect(in_part)
+    half_in, grad_down = lax.optimization_barrier((half_in, grad_down))
 
     own_gate = gate[:cap]
     mean_part = jnp.sum(half_in * own_rows.astype(F32), axis=1)

time: 203 us -> 206 us (1.015)
    ppermute x17, waiting for transfers between devices: 5.22 us -> 7.42 us  [swap_core(): return lax.ppermute(value, 'group', [(0, 1), (1, 0)])]
  transfers between devices with their start and end apart: 33 -> 33, of which waited for: 20 -> 21; matrix products, arithmetic and copies ran while one was open for 8% -> 8% of each run, Pallas kernels for 0% -> 0%
where the time goes in v3:
time: 206 us; the launch traced here: 205 us
  waiting for transfers between devices  86.4 us (42%)
  starting transfers between devices  49.2 us (24%)
  blocking collectives  19.2 us (9%)
  matrix products  17.8 us (9%)
  between operations  14.8 us (7%)
  local copies, waits for them, and re-layouts  8.07 us (4%)
  other arithmetic  6.66 us (3%)
  Pallas kernels  2.54 us (1%)
    ppermute x12, waiting for transfers between devices, hop(): return lax.ppermute(value, ('dp', 'group'), pairs)  49.1 us
    all_to_all x3, waiting for transfers between devices, exchange(): return lax.all_to_all(blocks, CHIPS, 0, 0)  29.3 us
    ppermute x17, starting transfers between devices, swap_core(): return lax.ppermute(value, 'group', [(0, 1), (1, 0)])  19.3 us
    all_to_all x1, blocking collectives, exchange(): return lax.all_to_all(blocks, CHIPS, 0, 0)  19.2 us
    ppermute x12, starting transfers between devices, hop(): return lax.ppermute(value, ('dp', 'group'), pairs)  16.9 us
    all_to_all x3, starting transfers between devices, exchange(): return lax.all_to_all(blocks, CHIPS, 0, 0)  13 us
    ppermute x17, waiting for transfers between devices, swap_core(): return lax.ppermute(value, 'group', [(0, 1), (1, 0)])  7.42 us
    dot_general x4, matrix products, contract_cols(): lax.dot_general(left, right, (((1,), (1,)), ((), ())), preferred_element_...  4.77 us
  transfers between devices with their start and end apart: 33, of which 21 were waited for; matrix products, arithmetic and copies ran while one was open for 8% of the time, Pallas kernels for 0%

profile of v3, /device:TPU:1, one launch (start us, length us, event | category | flops | bytes accessed | tf_op | source)
XLA Modules:
  0.0 204.7 jit_solution(2111362361070970947)
XLA Ops:
  7.2 0.9 copy.33
  8.7 0.7 multiply_add_fusion.1
  9.4 2.0 convolution_convert_fusion.4
  11.4 2.1 %convolution_convert_fusion.2 = bf16[128,4096]{1,0:T(8,128)(2,1)S(1)} fusion(bf16[128,256]{1,0:T(8,128)(2,1)} %param.11, bf16[256,4096]{1,0:T(8,128)(2,1)} %proj_ref.1), kind=kOutput, calls=%fused_computation.5 | convolution fusion | flops 268959744 | bytes 3211264 | tf_op jit(solution)/shard_map/dot_general | solution.py:137
  13.6 3.3 %collective-permute-start = (bf16[128,2048]{1,0:T(8,128)(2,1)S(1)}, bf16[128,2048]{1,0:T(8,128)(2,1)S(1)}, u32[]{:S(2)}, u32[]{:S(2)}) collective-permute-start(bf16[128,2048]{1,0:T(8,128)(2,1)S(1)} %constant_dynamic-slice_fusion.4), channel_id=1, source_target_pairs={{0,1},{1,0},{2,3},{3,2},{4,5},{5,4},{6,7},{7,6},{8,9},{9,8},{10,11... | collective-permute-start | bytes 1572872 | tf_op jit(solution)/shard_map/ppermute | solution.py:30
  16.9 1.5 collective-permute-done
  18.4 1.0 bitcast_bitcast_fusion
  19.4 5.2 %all-to-all-start = ((bf16[16,128,128]{2,1,0:T(8,128)(2,1)}), bf16[16,128,128]{2,1,0:T(8,128)(2,1)S(1)}, u32[]{:S(2)}, u32[]{:S(2)}) async-start(bf16[16,128,128]{2,1,0:T(8,128)(2,1)} %bitcast_bitcast_fusion), calls=%async_computation | async-start | bytes 1048576 | tf_op jit(solution)/shard_map/all_to_all | solution.py:44
  24.6 10.7 %all-to-all-done = bf16[16,128,128]{2,1,0:T(8,128)(2,1)S(1)} async-done(((bf16[16,128,128]{2,1,0:T(8,128)(2,1)}), bf16[16,128,128]{2,1,0:T(8,128)(2,1)S(1)}, u32[]{:S(2)}, u32[]{:S(2)}) %all-to-all-start) | async-done | bytes 524320 | tf_op jit(solution)/shard_map/all_to_all | solution.py:44
  35.3 0.8 fusion.35
  36.1 0.9 broadcast_in_dim.13
  37.0 3.6 %all-to-all-start.1 = ((bf16[16,128,128]{2,1,0:T(8,128)(2,1)}), bf16[16,128,128]{2,1,0:T(8,128)(2,1)S(1)}, u32[]{:S(2)}, u32[]{:S(2)}) async-start(bf16[16,128,128]{2,1,0:T(8,128)(2,1)} %broadcast_in_dim.13), calls=%async_computation.1 | async-start | bytes 1048576 | tf_op jit(solution)/shard_map/all_to_all | solution.py:44
  40.7 0.9 reduce-precision_convert_fusion.1
  41.7 8.9 %all-to-all-done.1 = bf16[16,128,128]{2,1,0:T(8,128)(2,1)S(1)} async-done(((bf16[16,128,128]{2,1,0:T(8,128)(2,1)}), bf16[16,128,128]{2,1,0:T(8,128)(2,1)S(1)}, u32[]{:S(2)}, u32[]{:S(2)}) %all-to-all-start.1) | async-done | bytes 524320 | tf_op jit(solution)/shard_map/all_to_all | solution.py:44
  50.9 2.6 %collective-permute-start.1 = (bf16[16,128,128]{1,2,0:T(8,128)(2,1)S(1)}, bf16[16,128,128]{1,2,0:T(8,128)(2,1)S(1)}, u32[]{:S(2)}, u32[]{:S(2)}) collective-permute-start(bf16[16,128,128]{1,2,0:T(8,128)(2,1)S(1)} %copy.36), channel_id=1, source_target_pairs={{0,1},{1,0},{2,3},{3,2},{4,5},{5,4},{6,7},{7,6},{8,9},{9,8},{10,11... | collective-permute-start | bytes 1572872 | tf_op jit(solution)/shard_map/ppermute | solution.py:30
  53.5 1.5 collective-permute-done.1
  55.0 0.6 fusion.1
  55.6 0.8 convolution_convert_fusion.3
  56.4 0.5 all-gather.3.cloned.1.call-done
  56.9 5.2 %collective-permute-start.2 = (bf16[48,4096]{1,0:T(8,128)(2,1)S(1)}, bf16[48,4096]{1,0:T(8,128)(2,1)S(1)}, u32[]{:S(2)}, u32[]{:S(2)}) collective-permute-start(bf16[48,4096]{1,0:T(8,128)(2,1)S(1)} %convolution_convert_fusion.3), channel_id=1, source_target_pairs={{0,32},{1,225},{32,64},{33,1},{64,96},{65,33},{96,128},{97,65},{12... | collective-permute-start | bytes 1179656 | tf_op jit(solution)/shard_map/ppermute | solution.py:40
  62.1 2.2 %dynamic-slice_bitcast_fusion.1 = (bf16[48,2048]{1,0:T(8,128)(2,1)S(1)}, bf16[48,2048]{1,0:T(8,128)(2,1)S(1)}, bf16[48,2048]{1,0:T(8,128)(2,1)S(1)}, bf16[48,204...) fusion(bf16[8,2,48,2048]{3,2,1,0:T(8,128)(2,1)} %bitcast.98, ...), kind=kLoop, calls=%fused_computation.77 | loop fusion | bytes 6291492 | tf_op jit(solution)/shard_map/squeeze | solution.py:164
  64.6 2.3 %collective-permute-done.2 = bf16[48,4096]{1,0:T(8,128)(2,1)S(1)} collective-permute-done((bf16[48,4096]{1,0:T(8,128)(2,1)S(1)}, bf16[48,4096]{1,0:T(8,128)(2,1)S(1)}, u32[]{:S(2)}, u32[]{:S(2)}) %collective-permute-start.2) | collective-permute-done | bytes 393248 | tf_op jit(solution)/shard_map/ppermute | solution.py:40
  66.8 3.1 %collective-permute-start.3 = (bf16[48,4096]{1,0:T(8,128)(2,1)S(1)}, bf16[48,4096]{1,0:T(8,128)(2,1)S(1)}, u32[]{:S(2)}, u32[]{:S(2)}) collective-permute-start(bf16[48,4096]{1,0:T(8,128)(2,1)S(1)} %collective-permute-done.2), channel_id=1, source_target_pairs={{0,32},{1,225},{32,64},{33,1},{64,96},{65,33},{96,128},{97,65},{12... | collective-permute-start | bytes 1179656 | tf_op jit(solution)/shard_map/ppermute | solution.py:40
  70.0 4.7 %collective-permute-done.3 = bf16[48,4096]{1,0:T(8,128)(2,1)S(1)} collective-permute-done((bf16[48,4096]{1,0:T(8,128)(2,1)S(1)}, bf16[48,4096]{1,0:T(8,128)(2,1)S(1)}, u32[]{:S(2)}, u32[]{:S(2)}) %collective-permute-start.3) | collective-permute-done | bytes 393248 | tf_op jit(solution)/shard_map/ppermute | solution.py:40
  74.7 3.1 %collective-permute-start.4 = (bf16[48,4096]{1,0:T(8,128)(2,1)S(1)}, bf16[48,4096]{1,0:T(8,128)(2,1)S(1)}, u32[]{:S(2)}, u32[]{:S(2)}) collective-permute-start(bf16[48,4096]{1,0:T(8,128)(2,1)S(1)} %collective-permute-done.3), channel_id=1, source_target_pairs={{0,32},{1,225},{32,64},{33,1},{64,96},{65,33},{96,128},{97,65},{12... | collective-permute-start | bytes 1179656 | tf_op jit(solution)/shard_map/ppermute | solution.py:40
  77.8 4.7 %collective-permute-done.4 = bf16[48,4096]{1,0:T(8,128)(2,1)S(1)} collective-permute-done((bf16[48,4096]{1,0:T(8,128)(2,1)S(1)}, bf16[48,4096]{1,0:T(8,128)(2,1)S(1)}, u32[]{:S(2)}, u32[]{:S(2)}) %collective-permute-start.4) | collective-permute-done | bytes 393248 | tf_op jit(solution)/shard_map/ppermute | solution.py:40
  82.5 3.2 %collective-permute-start.8 = (bf16[48,2048]{1,0:T(8,128)(2,1)S(1)}, bf16[48,2048]{1,0:T(8,128)(2,1)S(1)}, u32[]{:S(2)}, u32[]{:S(2)}) collective-permute-start(bf16[48,2048]{1,0:T(8,128)(2,1)S(1)} %constant_dynamic-slice_fusion.3), channel_id=1, source_target_pairs={{0,32},{1,225},{32,64},{33,1},{64,96},{65,33},{96,128},{97,65},{12... | collective-permute-start | bytes 589832 | tf_op jit(solution)/shard_map/ppermute | solution.py:40
  85.7 1.0 collective-permute-start.7
  86.8 1.5 collective-permute-done.8
  88.3 5.1 %collective-permute-start.9 = (bf16[48,2048]{1,0:T(8,128)(2,1)S(1)}, bf16[48,2048]{1,0:T(8,128)(2,1)S(1)}, u32[]{:S(2)}, u32[]{:S(2)}) collective-permute-start(bf16[48,2048]{1,0:T(8,128)(2,1)S(1)} %collective-permute-done.8), channel_id=1, source_target_pairs={{0,1},{1,0},{2,3},{3,2},{4,5},{5,4},{6,7},{7,6},{8,9},{9,8},{10,11... | collective-permute-start | bytes 589832 | tf_op jit(solution)/shard_map/ppermute | solution.py:30
  93.5 1.0 collective-permute-done.9
  94.7 1.2 fusion.12
  95.9 1.2 fusion.8
  97.1 0.9 convolution_reduce_fusion
  98.1 1.4 multiply_reduce_fusion.1
  99.5 1.0 convolution_convert_fusion
  100.7 0.5 collective-permute-start.10
  101.3 0.4 collective-permute-start.14
  101.8 1.1 fusion.10
  102.9 1.3 add_convert_fusion
  104.4 0.5 collective-permute-start.19
  104.9 2.5 %fusion = bf16[1,224,4096]{2,1,0:T(8,128)(2,1)} fusion(bf16[384,224]{0,1:T(8,128)(2,1)S(1)} %get-tuple-element.20, bf16[384,4096]{1,0:T(8,128)(2,1)S(1)} %maximum_dynamic-update-slice_fusion, f32[384]{0:T(512)S(1)} %add_divide_fusion.1), kind=kOutput, calls=%fused_computation.4 | convolution fusion | flops 710279168 | bytes 5154304 | tf_op jit(solution)/shard_map/dot_general | solution.py:14
  107.9 5.7 %collective-permute-done.20 = bf16[48,2048]{1,0:T(8,128)(2,1)S(1)} collective-permute-done((bf16[48,2048]{1,0:T(8,128)(2,1)S(1)}, bf16[48,2048]{1,0:T(8,128)(2,1)S(1)}, u32[]{:S(2)}, u32[]{:S(2)}) %collective-permute-start.20) | collective-permute-done | bytes 196640 | tf_op jit(solution)/shard_map/ppermute | solution.py:40
  114.2 5.6 %collective-permute-done.11 = bf16[48,2048]{1,0:T(8,128)(2,1)S(1)} collective-permute-done((bf16[48,2048]{1,0:T(8,128)(2,1)S(1)}, bf16[48,2048]{1,0:T(8,128)(2,1)S(1)}, u32[]{:S(2)}, u32[]{:S(2)}) %collective-permute-start.11) | collective-permute-done | bytes 196640 | tf_op jit(solution)/shard_map/ppermute | solution.py:40
  120.2 1.5 collective-permute-start.13
  121.7 6.1 %collective-permute-done.22 = bf16[48,4096]{1,0:T(8,128)(2,1)S(1)} collective-permute-done((bf16[48,4096]{1,0:T(8,128)(2,1)S(1)}, bf16[48,4096]{1,0:T(8,128)(2,1)S(1)}, u32[]{:S(2)}, u32[]{:S(2)}) %collective-permute-start.22) | collective-permute-done | bytes 393248 | tf_op jit(solution)/shard_map/ppermute | solution.py:40
  128.1 4.0 %collective-permute-done.13 = bf16[48,4096]{1,0:T(8,128)(2,1)S(1)} collective-permute-done((bf16[48,4096]{1,0:T(8,128)(2,1)S(1)}, bf16[48,4096]{1,0:T(8,128)(2,1)S(1)}, u32[]{:S(2)}, u32[]{:S(2)}) %collective-permute-start.13) | collective-permute-done | bytes 393248 | tf_op jit(solution)/shard_map/ppermute | solution.py:40
  132.3 4.0 %collective-permute-done.24 = bf16[48,4096]{1,0:T(8,128)(2,1)S(1)} collective-permute-done((bf16[48,4096]{1,0:T(8,128)(2,1)S(1)}, bf16[48,4096]{1,0:T(8,128)(2,1)S(1)}, u32[]{:S(2)}, u32[]{:S(2)}) %collective-permute-start.24) | collective-permute-done | bytes 393248 | tf_op jit(solution)/shard_map/ppermute | solution.py:40
  136.5 4.0 %collective-permute-done.15 = bf16[48,4096]{1,0:T(8,128)(2,1)S(1)} collective-permute-done((bf16[48,4096]{1,0:T(8,128)(2,1)S(1)}, bf16[48,4096]{1,0:T(8,128)(2,1)S(1)}, u32[]{:S(2)}, u32[]{:S(2)}) %collective-permute-start.15) | collective-permute-done | bytes 393248 | tf_op jit(solution)/shard_map/ppermute | solution.py:40
  140.7 4.0 %collective-permute-done.26 = bf16[48,4096]{1,0:T(8,128)(2,1)S(1)} collective-permute-done((bf16[48,4096]{1,0:T(8,128)(2,1)S(1)}, bf16[48,4096]{1,0:T(8,128)(2,1)S(1)}, u32[]{:S(2)}, u32[]{:S(2)}) %collective-permute-start.26) | collective-permute-done | bytes 393248 | tf_op jit(solution)/shard_map/ppermute | solution.py:40
  144.8 1.4 collective-permute-start.27
  146.1 2.8 %collective-permute-done.17 = bf16[48,4096]{1,0:T(8,128)(2,1)S(1)} collective-permute-done((bf16[48,4096]{1,0:T(8,128)(2,1)S(1)}, bf16[48,4096]{1,0:T(8,128)(2,1)S(1)}, u32[]{:S(2)}, u32[]{:S(2)}) %collective-permute-start.17) | collective-permute-done | bytes 393248 | tf_op jit(solution)/shard_map/ppermute | solution.py:40
  149.0 1.4 collective-permute-start.18
  150.7 1.0 collective-permute-done.18
  152.1 0.9 copy.38
  153.0 4.2 %all-to-all-start.2 = ((bf16[16,112,128]{2,1,0:T(8,128)(2,1)}), bf16[16,112,128]{2,1,0:T(8,128)(2,1)S(1)}, u32[]{:S(2)}, u32[]{:S(2)}) async-start(bf16[16,112,128]{2,1,0:T(8,128)(2,1)} %copy.38), calls=%async_computation.2 | async-start | bytes 917504 | tf_op jit(solution)/shard_map/all_to_all | solution.py:44
  157.5 9.7 %all-to-all-done.2 = bf16[16,112,128]{2,1,0:T(8,128)(2,1)S(1)} async-done(((bf16[16,112,128]{2,1,0:T(8,128)(2,1)}), bf16[16,112,128]{2,1,0:T(8,128)(2,1)S(1)}, u32[]{:S(2)}, u32[]{:S(2)}) %all-to-all-start.2) | async-done | bytes 458784 | tf_op jit(solution)/shard_map/all_to_all | solution.py:44
  167.5 1.1 fusion.17
  168.6 1.1 fusion.18
  169.9 19.2 %all_to_all.20.mine_ref = bf16[16,256,128]{2,1,0:T(8,128)(2,1)S(1)} all-to-all(bf16[16,256,128]{2,1,0:T(8,128)(2,1)S(1)} %broadcast_in_dim.17), channel_id=1, replica_groups=mesh['dp'=8,'y'=4,'xh'=2,'half'=2,'group'=2] {'y','xh','half'}, dimensions={0} | all-to-all | bytes 2097152 | tf_op jit(solution)/shard_map/all_to_all | solution.py:44
  189.0 2.4 %collective-permute-start.28 = (bf16[16,256,128]{2,1,0:T(8,128)(2,1)S(1)}, bf16[16,256,128]{2,1,0:T(8,128)(2,1)S(1)}, u32[]{:S(2)}, u32[]{:S(2)}) collective-permute-start(bf16[16,256,128]{2,1,0:T(8,128)(2,1)S(1)} %all_to_all.20.mine_ref), channel_id=1, source_target_pairs={{0,1},{1,0},{2,3},{3,2},{4,5},{5,4},{6,7},{7,6},{8,9},{9,8},{10,11... | collective-permute-start | bytes 3145736 | tf_op jit(solution)/shard_map/ppermute | solution.py:30
  191.4 2.3 %collective-permute-done.28.other_ref = bf16[16,256,128]{2,1,0:T(8,128)(2,1)S(1)} collective-permute-done((bf16[16,256,128]{2,1,0:T(8,128)(2,1)S(1)}, bf16[16,256,128]{2,1,0:T(8,128)(2,1)S(1)}, u32[]{:S(2)}, u32[]{:S(2)}) %collective-permute-start.28) | collective-permute-done | bytes 1048608 | tf_op jit(solution)/shard_map/ppermute | solution.py:30
  193.7 1.6 copy-done.2
  195.3 2.5 %shard_map.121 = (bf16[128,4096]{1,0:T(8,128)(2,1)}, bf16[128,256]{1,0:T(8,128)(2,1)}) custom-call(s32[1]{0:T(128)} %bitcast.core_ref, bf16[16,256,128]{2,1,0:T(8,128)(2,1)S(1)} %all_to_all.20.mine_ref, bf16[16,256,128]{2,1,0:T(8,128)(2,1)S(1)} %collective-permute-done.28.other_ref, bf16[256,4096]{1,0:T(8,128)(2,1)S(1)} %copy-done.2), custom_call_target="tpu_custom_call" | custom-call | tf_op jit(solution)/shard_map/pallas_call | solution.py:91
  (110 shorter events, 6.3 us)
Async XLA Ops:
  7.2 90.9 %copy-start = (bf16[1,224,4096]{2,1,0:T(8,128)(2,1)S(1)}, bf16[1,224,4096]{2,1,0:T(8,128)(2,1)}, u32[]{:S(2)}) copy-start(bf16[1,224,4096]{2,1,0:T(8,128)(2,1)} %param.18) | copy-start | bytes 5505028
  7.2 49.7 %all-gather.3.cloned.1.call-start = ((), (), s32[]{:S(2)}) async-start(), calls=%async_computation.4 | async-start | bytes 3342336 | tf_op jit(solution)/shard_map/all_gather | solution.py:136
  13.6 4.9 %collective-permute-start = (bf16[128,2048]{1,0:T(8,128)(2,1)S(1)}, bf16[128,2048]{1,0:T(8,128)(2,1)S(1)}, u32[]{:S(2)}, u32[]{:S(2)}) collective-permute-start(bf16[128,2048]{1,0:T(8,128)(2,1)S(1)} %constant_dynamic-slice_fusion.4), channel_id=1, source_target_pairs={{0,1},{1,0},{2,3},{3,2},{4,5},{5,4},{6,7},{7,6},{8,9},{9,8},{10,11... | collective-permute-start | bytes 1572872 | tf_op jit(solution)/shard_map/ppermute | solution.py:30
  19.4 36.2 %copy-start.6 = (f32[4096]{0:T(1024)S(1)}, f32[4096]{0:T(1024)}, u32[]{:S(2)}) copy-start(f32[4096]{0:T(1024)} %param.13) | copy-start | bytes 49156
  19.4 15.9 %all-to-all-start = ((bf16[16,128,128]{2,1,0:T(8,128)(2,1)}), bf16[16,128,128]{2,1,0:T(8,128)(2,1)S(1)}, u32[]{:S(2)}, u32[]{:S(2)}) async-start(bf16[16,128,128]{2,1,0:T(8,128)(2,1)} %bitcast_bitcast_fusion), calls=%async_computation | async-start | bytes 1048576 | tf_op jit(solution)/shard_map/all_to_all | solution.py:44
  37.0 13.6 %all-to-all-start.1 = ((bf16[16,128,128]{2,1,0:T(8,128)(2,1)}), bf16[16,128,128]{2,1,0:T(8,128)(2,1)S(1)}, u32[]{:S(2)}, u32[]{:S(2)}) async-start(bf16[16,128,128]{2,1,0:T(8,128)(2,1)} %broadcast_in_dim.13), calls=%async_computation.1 | async-start | bytes 1048576 | tf_op jit(solution)/shard_map/all_to_all | solution.py:44
  50.9 4.1 %collective-permute-start.1 = (bf16[16,128,128]{1,2,0:T(8,128)(2,1)S(1)}, bf16[16,128,128]{1,2,0:T(8,128)(2,1)S(1)}, u32[]{:S(2)}, u32[]{:S(2)}) collective-permute-start(bf16[16,128,128]{1,2,0:T(8,128)(2,1)S(1)} %copy.36), channel_id=1, source_target_pairs={{0,1},{1,0},{2,3},{3,2},{4,5},{5,4},{6,7},{7,6},{8,9},{9,8},{10,11... | collective-permute-start | bytes 1572872 | tf_op jit(solution)/shard_map/ppermute | solution.py:30
  56.9 9.9 %collective-permute-start.2 = (bf16[48,4096]{1,0:T(8,128)(2,1)S(1)}, bf16[48,4096]{1,0:T(8,128)(2,1)S(1)}, u32[]{:S(2)}, u32[]{:S(2)}) collective-permute-start(bf16[48,4096]{1,0:T(8,128)(2,1)S(1)} %convolution_convert_fusion.3), channel_id=1, source_target_pairs={{0,32},{1,225},{32,64},{33,1},{64,96},{65,33},{96,128},{97,65},{12... | collective-permute-start | bytes 1179656 | tf_op jit(solution)/shard_map/ppermute | solution.py:40
  64.6 30.1 %copy-start.4 = (bf16[1,4096,224]{1,2,0:T(8,128)(2,1)S(1)}, bf16[1,4096,224]{1,2,0:T(8,128)(2,1)}, u32[]{:S(2)}) copy-start(bf16[1,4096,224]{1,2,0:T(8,128)(2,1)} %param.16) | copy-start | bytes 5505028
  66.8 7.8 %collective-permute-start.3 = (bf16[48,4096]{1,0:T(8,128)(2,1)S(1)}, bf16[48,4096]{1,0:T(8,128)(2,1)S(1)}, u32[]{:S(2)}, u32[]{:S(2)}) collective-permute-start(bf16[48,4096]{1,0:T(8,128)(2,1)S(1)} %collective-permute-done.2), channel_id=1, source_target_pairs={{0,32},{1,225},{32,64},{33,1},{64,96},{65,33},{96,128},{97,65},{12... | collective-permute-start | bytes 1179656 | tf_op jit(solution)/shard_map/ppermute | solution.py:40
  70.0 16.8 %collective-permute-start.5 = (bf16[48,4096]{1,0:T(8,128)(2,1)S(1)}, bf16[48,4096]{1,0:T(8,128)(2,1)S(1)}, u32[]{:S(2)}, u32[]{:S(2)}) collective-permute-start(bf16[48,4096]{1,0:T(8,128)(2,1)S(1)} %collective-permute-done.2), channel_id=1, source_target_pairs={{0,1},{1,0},{2,3},{3,2},{4,5},{5,4},{6,7},{7,6},{8,9},{9,8},{10,11... | collective-permute-start | bytes 1179656 | tf_op jit(solution)/shard_map/ppermute | solution.py:30
  74.7 7.8 %collective-permute-start.4 = (bf16[48,4096]{1,0:T(8,128)(2,1)S(1)}, bf16[48,4096]{1,0:T(8,128)(2,1)S(1)}, u32[]{:S(2)}, u32[]{:S(2)}) collective-permute-start(bf16[48,4096]{1,0:T(8,128)(2,1)S(1)} %collective-permute-done.3), channel_id=1, source_target_pairs={{0,32},{1,225},{32,64},{33,1},{64,96},{65,33},{96,128},{97,65},{12... | collective-permute-start | bytes 1179656 | tf_op jit(solution)/shard_map/ppermute | solution.py:40
  77.8 9.0 %collective-permute-start.6 = (bf16[48,4096]{1,0:T(8,128)(2,1)S(1)}, bf16[48,4096]{1,0:T(8,128)(2,1)S(1)}, u32[]{:S(2)}, u32[]{:S(2)}) collective-permute-start(bf16[48,4096]{1,0:T(8,128)(2,1)S(1)} %collective-permute-done.3), channel_id=1, source_target_pairs={{0,1},{1,0},{2,3},{3,2},{4,5},{5,4},{6,7},{7,6},{8,9},{9,8},{10,11... | collective-permute-start | bytes 1179656 | tf_op jit(solution)/shard_map/ppermute | solution.py:30
  82.5 5.8 %collective-permute-start.8 = (bf16[48,2048]{1,0:T(8,128)(2,1)S(1)}, bf16[48,2048]{1,0:T(8,128)(2,1)S(1)}, u32[]{:S(2)}, u32[]{:S(2)}) collective-permute-start(bf16[48,2048]{1,0:T(8,128)(2,1)S(1)} %constant_dynamic-slice_fusion.3), channel_id=1, source_target_pairs={{0,32},{1,225},{32,64},{33,1},{64,96},{65,33},{96,128},{97,65},{12... | collective-permute-start | bytes 589832 | tf_op jit(solution)/shard_map/ppermute | solution.py:40
  85.7 7.8 %collective-permute-start.7 = (bf16[48,4096]{1,0:T(8,128)(2,1)S(1)}, bf16[48,4096]{1,0:T(8,128)(2,1)S(1)}, u32[]{:S(2)}, u32[]{:S(2)}) collective-permute-start(bf16[48,4096]{1,0:T(8,128)(2,1)S(1)} %collective-permute-done.4), channel_id=1, source_target_pairs={{0,1},{1,0},{2,3},{3,2},{4,5},{5,4},{6,7},{7,6},{8,9},{9,8},{10,11... | collective-permute-start | bytes 1179656 | tf_op jit(solution)/shard_map/ppermute | solution.py:30
  88.3 6.2 %collective-permute-start.9 = (bf16[48,2048]{1,0:T(8,128)(2,1)S(1)}, bf16[48,2048]{1,0:T(8,128)(2,1)S(1)}, u32[]{:S(2)}, u32[]{:S(2)}) collective-permute-start(bf16[48,2048]{1,0:T(8,128)(2,1)S(1)} %collective-permute-done.8), channel_id=1, source_target_pairs={{0,1},{1,0},{2,3},{3,2},{4,5},{5,4},{6,7},{7,6},{8,9},{9,8},{10,11... | collective-permute-start | bytes 589832 | tf_op jit(solution)/shard_map/ppermute | solution.py:30
  93.5 2.4 %copy-start.3 = (bf16[1,4096,224]{1,2,0:T(8,128)(2,1)S(1)}, bf16[1,4096,224]{1,2,0:T(8,128)(2,1)}, u32[]{:S(2)}) copy-start(bf16[1,4096,224]{1,2,0:T(8,128)(2,1)} %param.17) | copy-start | bytes 5505028
  98.1 6.8 %copy-start.5 = (f32[384]{0:T(512)}, f32[384]{0:T(512)S(1)}, u32[]{:S(2)}) copy-start(f32[384]{0:T(512)S(1)} %add_divide_fusion.1) | copy-start | bytes 4612
  100.7 6.8 %collective-permute-start.10 = (bf16[48,2048]{1,0:T(8,128)(2,1)S(1)}, bf16[48,2048]{1,0:T(8,128)(2,1)S(1)}, u32[]{:S(2)}, u32[]{:S(2)}) collective-permute-start(bf16[48,2048]{1,0:T(8,128)(2,1)S(1)} %constant_dynamic-slice_fusion.1), channel_id=1, source_target_pairs={{0,1},{1,0},{2,3},{3,2},{4,5},{5,4},{6,7},{7,6},{8,9},{9,8},{10,11... | collective-permute-start | bytes 589832 | tf_op jit(solution)/shard_map/ppermute | solution.py:30
  101.2 18.7 %collective-permute-start.12 = (bf16[48,4096]{1,0:T(8,128)(2,1)S(1)}, bf16[48,4096]{1,0:T(8,128)(2,1)S(1)}, u32[]{:S(2)}, u32[]{:S(2)}) collective-permute-start(bf16[48,4096]{1,0:T(8,128)(2,1)S(1)} %get-tuple-element.26), channel_id=1, source_target_pairs={{0,1},{1,0},{2,3},{3,2},{4,5},{5,4},{6,7},{7,6},{8,9},{9,8},{10,11... | collective-permute-start | bytes 1179656 | tf_op jit(solution)/shard_map/ppermute | solution.py:30
  101.3 26.8 %collective-permute-start.14 = (bf16[48,4096]{1,0:T(8,128)(2,1)S(1)}, bf16[48,4096]{1,0:T(8,128)(2,1)S(1)}, u32[]{:S(2)}, u32[]{:S(2)}) collective-permute-start(bf16[48,4096]{1,0:T(8,128)(2,1)S(1)} %get-tuple-element.25), channel_id=1, source_target_pairs={{0,1},{1,0},{2,3},{3,2},{4,5},{5,4},{6,7},{7,6},{8,9},{9,8},{10,11... | collective-permute-start | bytes 1179656 | tf_op jit(solution)/shard_map/ppermute | solution.py:30
  101.7 34.8 %collective-permute-start.16 = (bf16[48,4096]{1,0:T(8,128)(2,1)S(1)}, bf16[48,4096]{1,0:T(8,128)(2,1)S(1)}, u32[]{:S(2)}, u32[]{:S(2)}) collective-permute-start(bf16[48,4096]{1,0:T(8,128)(2,1)S(1)} %get-tuple-element.24), channel_id=1, source_target_pairs={{0,1},{1,0},{2,3},{3,2},{4,5},{5,4},{6,7},{7,6},{8,9},{9,8},{10,11... | collective-permute-start | bytes 1179656 | tf_op jit(solution)/shard_map/ppermute | solution.py:30
  104.4 2.9 %collective-permute-start.19 = (bf16[48,2048]{1,0:T(8,128)(2,1)S(1)}, bf16[48,2048]{1,0:T(8,128)(2,1)S(1)}, u32[]{:S(2)}, u32[]{:S(2)}) collective-permute-start(bf16[48,2048]{1,0:T(8,128)(2,1)S(1)} %constant_dynamic-slice_fusion), channel_id=1, source_target_pairs={{0,1},{1,0},{2,3},{3,2},{4,5},{5,4},{6,7},{7,6},{8,9},{9,8},{10,11... | collective-permute-start | bytes 589832 | tf_op jit(solution)/shard_map/ppermute | solution.py:30
  107.3 6.6 %collective-permute-start.21 = (bf16[48,4096]{1,0:T(8,128)(2,1)S(1)}, bf16[48,4096]{1,0:T(8,128)(2,1)S(1)}, u32[]{:S(2)}, u32[]{:S(2)}) collective-permute-start(bf16[48,4096]{1,0:T(8,128)(2,1)S(1)} %get-tuple-element.30), channel_id=1, source_target_pairs={{0,1},{1,0},{2,3},{3,2},{4,5},{5,4},{6,7},{7,6},{8,9},{9,8},{10,11... | collective-permute-start | bytes 1179656 | tf_op jit(solution)/shard_map/ppermute | solution.py:30
  107.5 6.0 %collective-permute-start.20 = (bf16[48,2048]{1,0:T(8,128)(2,1)S(1)}, bf16[48,2048]{1,0:T(8,128)(2,1)S(1)}, u32[]{:S(2)}, u32[]{:S(2)}) collective-permute-start(bf16[48,2048]{1,0:T(8,128)(2,1)S(1)} %add_convert_fusion.10), channel_id=1, source_target_pairs={{0,224},{1,33},{32,0},{33,65},{64,32},{65,97},{96,64},{97,129},{12... | collective-permute-start | bytes 589832 | tf_op jit(solution)/shard_map/ppermute | solution.py:40
  113.6 6.6 %collective-permute-start.23 = (bf16[48,4096]{1,0:T(8,128)(2,1)S(1)}, bf16[48,4096]{1,0:T(8,128)(2,1)S(1)}, u32[]{:S(2)}, u32[]{:S(2)}) collective-permute-start(bf16[48,4096]{1,0:T(8,128)(2,1)S(1)} %get-tuple-element.29), channel_id=1, source_target_pairs={{0,1},{1,0},{2,3},{3,2},{4,5},{5,4},{6,7},{7,6},{8,9},{9,8},{10,11... | collective-permute-start | bytes 1179656 | tf_op jit(solution)/shard_map/ppermute | solution.py:30
  113.9 5.8 %collective-permute-start.11 = (bf16[48,2048]{1,0:T(8,128)(2,1)S(1)}, bf16[48,2048]{1,0:T(8,128)(2,1)S(1)}, u32[]{:S(2)}, u32[]{:S(2)}) collective-permute-start(bf16[48,2048]{1,0:T(8,128)(2,1)S(1)} %add_convert_fusion.11), channel_id=1, source_target_pairs={{0,224},{1,33},{32,0},{33,65},{64,32},{65,97},{96,64},{97,129},{12... | collective-permute-start | bytes 589832 | tf_op jit(solution)/shard_map/ppermute | solution.py:40
  119.7 12.6 %collective-permute-start.25 = (bf16[48,4096]{1,0:T(8,128)(2,1)S(1)}, bf16[48,4096]{1,0:T(8,128)(2,1)S(1)}, u32[]{:S(2)}, u32[]{:S(2)}) collective-permute-start(bf16[48,4096]{1,0:T(8,128)(2,1)S(1)} %get-tuple-element.28), channel_id=1, source_target_pairs={{0,1},{1,0},{2,3},{3,2},{4,5},{5,4},{6,7},{7,6},{8,9},{9,8},{10,11... | collective-permute-start | bytes 1179656 | tf_op jit(solution)/shard_map/ppermute | solution.py:30
  119.9 7.9 %collective-permute-start.22 = (bf16[48,4096]{1,0:T(8,128)(2,1)S(1)}, bf16[48,4096]{1,0:T(8,128)(2,1)S(1)}, u32[]{:S(2)}, u32[]{:S(2)}) collective-permute-start(bf16[48,4096]{1,0:T(8,128)(2,1)S(1)} %add_convert_fusion.5), channel_id=1, source_target_pairs={{0,224},{1,33},{32,0},{33,65},{64,32},{65,97},{96,64},{97,129},{12... | collective-permute-start | bytes 1179656 | tf_op jit(solution)/shard_map/ppermute | solution.py:40
  120.2 11.9 %collective-permute-start.13 = (bf16[48,4096]{1,0:T(8,128)(2,1)S(1)}, bf16[48,4096]{1,0:T(8,128)(2,1)S(1)}, u32[]{:S(2)}, u32[]{:S(2)}) collective-permute-start(bf16[48,4096]{1,0:T(8,128)(2,1)S(1)} %add_convert_fusion.9), channel_id=1, source_target_pairs={{0,224},{1,33},{32,0},{33,65},{64,32},{65,97},{96,64},{97,129},{12... | collective-permute-start | bytes 1179656 | tf_op jit(solution)/shard_map/ppermute | solution.py:40
  128.0 8.3 %collective-permute-start.24 = (bf16[48,4096]{1,0:T(8,128)(2,1)S(1)}, bf16[48,4096]{1,0:T(8,128)(2,1)S(1)}, u32[]{:S(2)}, u32[]{:S(2)}) collective-permute-start(bf16[48,4096]{1,0:T(8,128)(2,1)S(1)} %add_convert_fusion.4), channel_id=1, source_target_pairs={{0,224},{1,33},{32,0},{33,65},{64,32},{65,97},{96,64},{97,129},{12... | collective-permute-start | bytes 1179656 | tf_op jit(solution)/shard_map/ppermute | solution.py:40
  132.2 8.3 %collective-permute-start.15 = (bf16[48,4096]{1,0:T(8,128)(2,1)S(1)}, bf16[48,4096]{1,0:T(8,128)(2,1)S(1)}, u32[]{:S(2)}, u32[]{:S(2)}) collective-permute-start(bf16[48,4096]{1,0:T(8,128)(2,1)S(1)} %add_convert_fusion.8), channel_id=1, source_target_pairs={{0,224},{1,33},{32,0},{33,65},{64,32},{65,97},{96,64},{97,129},{12... | collective-permute-start | bytes 1179656 | tf_op jit(solution)/shard_map/ppermute | solution.py:40
  136.4 8.3 %collective-permute-start.26 = (bf16[48,4096]{1,0:T(8,128)(2,1)S(1)}, bf16[48,4096]{1,0:T(8,128)(2,1)S(1)}, u32[]{:S(2)}, u32[]{:S(2)}) collective-permute-start(bf16[48,4096]{1,0:T(8,128)(2,1)S(1)} %add_convert_fusion.3), channel_id=1, source_target_pairs={{0,224},{1,33},{32,0},{33,65},{64,32},{65,97},{96,64},{97,129},{12... | collective-permute-start | bytes 1179656 | tf_op jit(solution)/shard_map/ppermute | solution.py:40
  140.6 11.1 %slice-start = ((f32[384]{0:T(512)}), f32[48]{0:T(128)S(1)}, s32[]{:S(2)}) async-start(f32[384]{0:T(512)} %copy-done.5), calls=%async_computation.5 | async-start | bytes 1024 | tf_op jit(solution)/shard_map/slice | solution.py:206
  140.6 8.3 %collective-permute-start.17 = (bf16[48,4096]{1,0:T(8,128)(2,1)S(1)}, bf16[48,4096]{1,0:T(8,128)(2,1)S(1)}, u32[]{:S(2)}, u32[]{:S(2)}) collective-permute-start(bf16[48,4096]{1,0:T(8,128)(2,1)S(1)} %add_convert_fusion.7), channel_id=1, source_target_pairs={{0,224},{1,33},{32,0},{33,65},{64,32},{65,97},{96,64},{97,129},{12... | collective-permute-start | bytes 1179656 | tf_op jit(solution)/shard_map/ppermute | solution.py:40
  144.8 5.6 %collective-permute-start.27 = (bf16[48,4096]{1,0:T(8,128)(2,1)S(1)}, bf16[48,4096]{1,0:T(8,128)(2,1)S(1)}, u32[]{:S(2)}, u32[]{:S(2)}) collective-permute-start(bf16[48,4096]{1,0:T(8,128)(2,1)S(1)} %add_convert_fusion.2), channel_id=1, source_target_pairs={{0,1},{1,0},{2,3},{3,2},{4,5},{5,4},{6,7},{7,6},{8,9},{9,8},{10,11... | collective-permute-start | bytes 1179656 | tf_op jit(solution)/shard_map/ppermute | solution.py:30
  149.0 2.7 %collective-permute-start.18 = (bf16[48,4096]{1,0:T(8,128)(2,1)S(1)}, bf16[48,4096]{1,0:T(8,128)(2,1)S(1)}, u32[]{:S(2)}, u32[]{:S(2)}) collective-permute-start(bf16[48,4096]{1,0:T(8,128)(2,1)S(1)} %add_convert_fusion.6), channel_id=1, source_target_pairs={{0,1},{1,0},{2,3},{3,2},{4,5},{5,4},{6,7},{7,6},{8,9},{9,8},{10,11... | collective-permute-start | bytes 1179656 | tf_op jit(solution)/shard_map/ppermute | solution.py:30
  153.0 14.2 %all-to-all-start.2 = ((bf16[16,112,128]{2,1,0:T(8,128)(2,1)}), bf16[16,112,128]{2,1,0:T(8,128)(2,1)S(1)}, u32[]{:S(2)}, u32[]{:S(2)}) async-start(bf16[16,112,128]{2,1,0:T(8,128)(2,1)} %copy.38), calls=%async_computation.2 | async-start | bytes 917504 | tf_op jit(solution)/shard_map/all_to_all | solution.py:44
  169.7 28.2 %copy-start.1 = (bf16[1,224,4096]{2,1,0:T(8,128)(2,1)S(1)}, bf16[1,224,4096]{2,1,0:T(8,128)(2,1)}, u32[]{:S(2)}) copy-start(bf16[1,224,4096]{2,1,0:T(8,128)(2,1)} %param.18) | copy-start | bytes 5505028
  189.0 4.7 %collective-permute-start.28 = (bf16[16,256,128]{2,1,0:T(8,128)(2,1)S(1)}, bf16[16,256,128]{2,1,0:T(8,128)(2,1)S(1)}, u32[]{:S(2)}, u32[]{:S(2)}) collective-permute-start(bf16[16,256,128]{2,1,0:T(8,128)(2,1)S(1)} %all_to_all.20.mine_ref), channel_id=1, source_target_pairs={{0,1},{1,0},{2,3},{3,2},{4,5},{5,4},{6,7},{7,6},{8,9},{9,8},{10,11... | collective-permute-start | bytes 3145736 | tf_op jit(solution)/shard_map/ppermute | solution.py:30
  193.7 1.6 copy-start.2
Sparse Core Ops, SparseCore 0:
  11.6 45.2 all-gather.2
